TPU v7x, 32 devices: a whole 2x2x4 slice. The times are simulated.
32 devices in a mesh: grp: 4 (over z), gx: 2 (over y), gy: 4 (over x, core).
Axes of the slice: x: 2, y: 2, z: 4, core: 2. Of those that a mesh axis runs over, the one named last changes fastest.
Arguments:
- states: bfloat16 [12, 32, 64, 512], P(None, 'gx', 'gy', 'grp'), may hold values from 0 to 1
- membrane: float32 [32, 64, 512], P('gx', 'gy', 'grp'), may hold values from -3 to 3
- phi_heart: float32 [32, 64, 512], P('gx', 'gy', 'grp'), may hold values from -3 to 3
- ion_params: float32 [5, 12], replicated, may hold values from -1.5 to 20, as said below
- torso_phi: float32 [32, 128, 512], P('gx', 'gy', 'grp'), may hold values from -3 to 3
- tissue_scale: float32 [32, 128, 512], P('gx', 'gy', 'grp'), may hold values from 0.5 to 2
- labels: int32 [32, 128, 512], P('gx', 'gy', 'grp'), may hold values from 0 to 3
- cond_table: float32 [4], replicated, may hold values from 0.1 to 2
- send_node: int32 [4, 2, 4, 8, 512], P('grp', 'gx', 'gy'), may hold values from 0 to 8191
- send_count: int32 [4, 2, 4, 8], P('grp', 'gx', 'gy'), may hold values from 64 to 512, as said below
- recv_voxel: int32 [4, 2, 4, 8, 512], P('grp', 'gx', 'gy'), may hold values from 0 to 16383
- recv_count: int32 [4, 2, 4, 8], P('grp', 'gx', 'gy'), may hold values from 64 to 512, as said below
Outputs:
- new_membrane: float32 [32, 64, 512], P('gx', 'gy', 'grp')
- heart_phi: float32 [32, 64, 512], P('gx', 'gy', 'grp')
- torso_out: float32 [32, 128, 512], P('gx', 'gy', 'grp')
Inputs may be any that keep to these rules, and one draw needn't show every extreme that they name: `ion_params`: rows are midpoints in -1 to 1, slopes in 0.1 to 0.5, relaxation rates in 0.5 to 20, conductances in 0.1 to 0.6 and reversal potentials in -1.5 to 1.5, one column per state. send_count[g, i, j, p] is the number of live slots, from the first on, of the patch that device (g, i, j) sends to peer p of its slab; every device sends exactly 512 to one peer. recv_count[g, i, j, s] equals send_count of peer s of slab g for peer i * 4 + j; every device receives exactly 512 from one peer.
All inputs are finite; a program needn't handle non-finite values.
Results may differ from a plain program's by a relative error of at most 0.0003.
Values sent between devices are 32-bit elements; how exact they have to be, the bound alone decides.
A program may use at most 128 MiB of HBM per device.

v0:
```python
import math

import jax
import jax.numpy as jnp
from jax import lax
from jax.sharding import PartitionSpec as P

LABELS = 4
SWEEPS_H = 3
SWEEPS_T = 4


time_step = 0.1
intra_cond = 0.25
extra_cond = 0.5
penalty = 2.0
cheb_low = 0.1
cheb_high = 2.0


def with_halo(cells, sides, width):
    for axis, dim in sides:
        count = lax.axis_size(axis)
        head = lax.slice_in_dim(cells, 0, width, axis=dim)
        tail = lax.slice_in_dim(cells, cells.shape[dim] - width, cells.shape[dim], axis=dim)
        cells = jnp.concatenate(
            [
                lax.ppermute(tail, axis, [(i, (i + 1) % count) for i in range(count)]),
                cells,
                lax.ppermute(head, axis, [((i + 1) % count, i) for i in range(count)]),
            ],
            axis=dim,
        )
    return cells


def cheb_coeffs(sweeps):
    centre = 0.5 * (cheb_high + cheb_low)
    half_width = 0.5 * (cheb_high - cheb_low)
    scaled = centre / half_width
    coeffs = [(0.0, 1.0 / centre)]
    rho_old = 1.0 / scaled
    for number in range(1, sweeps):
        rho_new = 1.0 / (2.0 * scaled - rho_old)
        coeffs.append((rho_new * rho_old, 2.0 * rho_new / half_width))
        rho_old = rho_new
    return coeffs


def face_mask(cell_count, margin, start_at, whole):
    positions = start_at + jnp.arange(cell_count + 2 * margin, dtype=jnp.int32) - margin
    return ((positions >= 0) & (positions + 1 <= whole - 1)).astype(jnp.float32)


def harmonic(lower_cell, upper_cell):
    return 2.0 * lower_cell * upper_cell / (lower_cell + upper_cell)


def faces_from(conduct, mask_x, mask_y, mask_z):
    face_x = (
        jnp.concatenate([harmonic(conduct[:-1], conduct[1:]), jnp.zeros_like(conduct[:1])], 0)
        * mask_x[:, None, None]
    )
    face_y = (
        jnp.concatenate(
            [harmonic(conduct[:, :-1], conduct[:, 1:]), jnp.zeros_like(conduct[:, :1])], 1
        )
        * mask_y[None, :, None]
    )
    face_z = (
        jnp.concatenate(
            [harmonic(conduct[:, :, :-1], conduct[:, :, 1:]), jnp.zeros_like(conduct[:, :, :1])], 2
        )
        * mask_z[None, None, :]
    )
    return (face_x, face_y, face_z)


def flux_sum(values, conductances):
    face_x, face_y, face_z = conductances
    along_x = face_x[:-1] * (values[1:] - values[:-1])
    along_y = face_y[:, :-1] * (values[:, 1:] - values[:, :-1])
    along_z = face_z[:, :, :-1] * (values[:, :, 1:] - values[:, :, :-1])
    summed = (along_x[:-1] - along_x[1:])[:, 1:-1, 1:-1]
    summed = summed + (along_y[:, :-1] - along_y[:, 1:])[1:-1, :, 1:-1]
    return summed + (along_z[:, :, :-1] - along_z[:, :, 1:])[1:-1, 1:-1, :]


def face_total(conductances):
    face_x, face_y, face_z = conductances
    summed = (face_x[:-2] + face_x[1:-1])[:, 1:-1, 1:-1]
    summed = summed + (face_y[:, :-2] + face_y[:, 1:-1])[1:-1, :, 1:-1]
    return summed + (face_z[:, :, :-2] + face_z[:, :, 1:-1])[1:-1, 1:-1, :]


def trim_by(values, amount):
    if amount == 0:
        return values
    return values[amount:-amount, amount:-amount, amount:-amount]


def trim_faces(conductances, amount):
    return (
        trim_by(conductances[0], amount),
        trim_by(conductances[1], amount),
        trim_by(conductances[2], amount),
    )


def lookup(labels, cond_table):
    picked = jnp.zeros(labels.shape, jnp.float32)
    for number in range(LABELS):
        picked = picked + jnp.where(
            labels == number, cond_table[number], jnp.zeros((), jnp.float32)
        )
    return picked


def ionic_current(states, membrane, ion_params):
    params_col = ion_params[:, :, None, None, None]
    gate_vals = states.astype(jnp.float32)
    voltage = membrane[None]
    steady = jax.nn.sigmoid((voltage - params_col[0]) / params_col[1])
    gate_vals = steady + (gate_vals - steady) * jnp.exp(-time_step * params_col[2])
    return jnp.sum(params_col[3] * gate_vals * (voltage - params_col[4]), axis=0)


def local_faces(conduct_ext, grid_shape, margin):
    mask_x = jnp.ones((grid_shape[0] + 2 * margin,), jnp.float32)
    mask_y = face_mask(
        grid_shape[1],
        margin,
        lax.axis_index("gy") * grid_shape[1],
        grid_shape[1] * lax.axis_size("gy"),
    )
    mask_z = face_mask(
        grid_shape[2],
        margin,
        lax.axis_index("grp") * grid_shape[2],
        grid_shape[2] * lax.axis_size("grp"),
    )
    return faces_from(conduct_ext, mask_x, mask_y, mask_z)


def slot_block(total, slot_cap):
    return math.gcd(total // slot_cap, max(1, 4096 // slot_cap)) * slot_cap


def gather_cells(table, index, block):
    row_count, width = table.shape
    row_ids = jnp.arange(row_count, dtype=jnp.int32)
    col_ids = jnp.arange(width, dtype=jnp.int32)

    def gather_one_block(indices):
        row_hot = (indices[:, None] // width == row_ids[None, :]).astype(jnp.float32)
        chosen = jnp.dot(
            row_hot, table, precision=lax.Precision.HIGHEST, preferred_element_type=jnp.float32
        )
        return jnp.sum(
            jnp.where(
                indices[:, None] % width == col_ids[None, :], chosen, jnp.zeros((), jnp.float32)
            ),
            axis=1,
        )

    return lax.map(gather_one_block, index.reshape(-1, block)).reshape(index.shape)


def scatter_cells(values, index, row_count, width, block):
    row_ids = jnp.arange(row_count, dtype=jnp.int32)
    col_ids = jnp.arange(width, dtype=jnp.int32)
    count = len(values)
    stacked = jnp.stack([item.reshape(-1, block) for item in values], axis=1)

    def scatter_one_block(total, pieces):
        indices, weights = pieces
        row_hot = (indices[:, None] // width == row_ids[None, :]).astype(jnp.float32)
        col_hot = (indices[:, None] % width == col_ids[None, :]).astype(jnp.float32)
        weighted = jnp.concatenate(
            [weights[number][:, None] * col_hot for number in range(count)], axis=1
        )
        total = total + lax.dot_general(
            row_hot,
            weighted,
            (((0,), (0,)), ((), ())),
            precision=lax.Precision.HIGHEST,
            preferred_element_type=jnp.float32,
        )
        return (total, None)

    start = jnp.zeros((row_count, width * count), jnp.float32)
    total, unused = lax.scan(scatter_one_block, start, (index.reshape(-1, block), stacked))
    return [total[:, number * width : (number + 1) * width] for number in range(count)]


def widen_surface(surface, grid_shape):
    layer = surface.reshape(grid_shape[0] // 4, grid_shape[1], grid_shape[2])
    rest = jnp.zeros(
        (grid_shape[0] - grid_shape[0] // 4, grid_shape[1], grid_shape[2]), jnp.float32
    )
    return jnp.concatenate([layer, rest], axis=0)


def per_device(
    states,
    membrane,
    phi_heart,
    ion_params,
    torso_phi,
    tissue_scale,
    labels,
    cond_table,
    send_node,
    send_count,
    recv_voxel,
    recv_count,
):
    heart_shape = membrane.shape
    torso_shape = torso_phi.shape
    peer_count = lax.axis_size("gx") * lax.axis_size("gy")
    heart_coeffs = cheb_coeffs(SWEEPS_H)
    heart_depth = SWEEPS_H + 1
    deep_rim = with_halo(
        jnp.stack([membrane, phi_heart]), (("grp", 3), ("gx", 1), ("gy", 2)), heart_depth
    )
    wide_shape = (
        heart_shape[0] + 2 * heart_depth,
        heart_shape[1] + 2 * heart_depth,
        heart_shape[2] + 2 * heart_depth,
    )
    wide_faces = local_faces(jnp.ones(wide_shape, jnp.float32), heart_shape, heart_depth)
    total_ext = (intra_cond + extra_cond) * face_total(wide_faces)
    lap_mem_ext = flux_sum(deep_rim[0], wide_faces)
    source_ext = -intra_cond * lap_mem_ext
    iterate = deep_rim[1]
    update = jnp.zeros_like(iterate)
    for number, (carry_coef, resid_coef) in enumerate(heart_coeffs):
        residue = (
            trim_by(source_ext, number)
            - (intra_cond + extra_cond) * flux_sum(iterate, trim_faces(wide_faces, number))
        ) / trim_by(total_ext, number)
        update = carry_coef * trim_by(update, 1) + resid_coef * residue
        iterate = trim_by(iterate, 1) + update
    lap_phi = flux_sum(iterate, trim_faces(wide_faces, SWEEPS_H))
    phi_new = trim_by(iterate, 1)
    lap_membrane = trim_by(lap_mem_ext, heart_depth - 1)
    heart_total = trim_by(total_ext, heart_depth - 1)
    current = ionic_current(states, membrane, ion_params)
    new_membrane = membrane + time_step * (-intra_cond * (lap_membrane + lap_phi) - current)
    slot_cap = send_node.shape[-1]
    slot_total = peer_count * slot_cap
    block = slot_block(slot_total, slot_cap)
    slot_ids = jnp.arange(slot_cap, dtype=jnp.int32)
    node_map = send_node.reshape(peer_count, -1)
    sender_live = slot_ids[None, :] < send_count.reshape(peer_count, 1)
    heart_rows = heart_shape[0] // 4 * heart_shape[1]
    heart_table = phi_new[: heart_shape[0] // 4].reshape(heart_rows, heart_shape[2])
    picked_heart = gather_cells(heart_table, node_map.reshape(-1), block).reshape(peer_count, -1)
    sent_vals = jnp.where(sender_live, picked_heart, jnp.zeros((), jnp.float32))
    arrived = lax.all_to_all(sent_vals, ("gx", "gy"), split_axis=0, concat_axis=0, tiled=True)
    voxel_map = recv_voxel.reshape(peer_count, -1)
    receiver_live = slot_ids[None, :] < recv_count.reshape(peer_count, 1)
    live_weight = receiver_live.astype(jnp.float32) * penalty
    torso_rows = torso_shape[0] // 4 * torso_shape[1]
    right_surface, weight_surface = scatter_cells(
        (live_weight * arrived, live_weight),
        voxel_map.reshape(-1),
        torso_rows,
        torso_shape[2],
        block,
    )
    right_side = widen_surface(right_surface, torso_shape)
    weight = widen_surface(weight_surface, torso_shape)
    conduct = tissue_scale * lookup(labels, cond_table)
    coeffs = cheb_coeffs(SWEEPS_T)
    conduct_ext = with_halo(conduct[None], (("grp", 3), ("gx", 1), ("gy", 2)), 1)[0]
    conductances = local_faces(conduct_ext, torso_shape, 1)
    diagonal = face_total(conductances) + weight
    iterate = torso_phi
    update = jnp.zeros_like(iterate)
    for carry_coef, resid_coef in coeffs:
        extended = with_halo(iterate[None], (("grp", 3), ("gx", 1), ("gy", 2)), 1)[0]
        residue = (right_side - (flux_sum(extended, conductances) + weight * iterate)) / diagonal
        update = carry_coef * update + resid_coef * residue
        iterate = iterate + update
    torso_table = iterate[: torso_shape[0] // 4].reshape(torso_rows, torso_shape[2])
    picked_torso = gather_cells(torso_table, voxel_map.reshape(-1), block).reshape(peer_count, -1)
    returned = jnp.where(
        receiver_live, penalty * (arrived - picked_torso), jnp.zeros((), jnp.float32)
    )
    came_back = lax.all_to_all(returned, ("gx", "gy"), split_axis=0, concat_axis=0, tiled=True)
    live_back = jnp.where(sender_live, came_back, jnp.zeros((), jnp.float32))
    flux_surface = scatter_cells(
        (live_back,), node_map.reshape(-1), heart_rows, heart_shape[2], block
    )[0]
    flux_in = widen_surface(flux_surface, heart_shape)
    heart_phi = phi_new - flux_in / heart_total
    return (new_membrane, heart_phi, iterate)


def solution(mesh):
    placed = (
        P(None, "gx", "gy", "grp"),
        P("gx", "gy", "grp"),
        P("gx", "gy", "grp"),
        P(),
        P("gx", "gy", "grp"),
        P("gx", "gy", "grp"),
        P("gx", "gy", "grp"),
        P(),
        P("grp", "gx", "gy", None, None),
        P("grp", "gx", "gy", None),
        P("grp", "gx", "gy", None, None),
        P("grp", "gx", "gy", None),
    )
    return jax.shard_map(
        per_device,
        mesh=mesh,
        in_specs=placed,
        out_specs=(P("gx", "gy", "grp"), P("gx", "gy", "grp"), P("gx", "gy", "grp")),
        check_vma=False,
    )
```

profile of v0, /device:TPU:0, one launch (start us, length us, event | category | flops | bytes accessed | tf_op | source)
XLA Modules:
  0.0 178.9 jit_solution(5451121527714418011)
XLA Ops:
  1.9 5.1 %collective-permute-start.1 = (f32[2,16,16,4]{3,2,1,0:T(8,128)S(1)}, f32[2,16,16,4]{3,2,1,0:T(8,128)S(1)}, u32[]{:S(2)}, u32[]{:S(2)}) collective-permute-start(f32[2,16,16,4]{3,2,1,0:T(8,128)S(1)} %get-tuple-element.210), channel_id=1, source_target_pairs={{8,0},{16,8},{24,16},{0,24},{9,1},{17,9},{25,17},{1,25},{10,2},{18... | collective-permute-start | bytes 24584 | tf_op jit(solution)/shard_map/ppermute | solution.py:30
  8.4 3.6 %multiply_bitcast_fusion = f32[1,16,32,128]{3,2,1,0:T(8,128)S(1)} fusion(f32[16,32,128]{2,1,0:T(8,128)} %param.17, s32[16,32,128]{2,1,0:T(8,128)} %param.18, f32[]{:T(128)} %bitcast.20, f32[]{:T(128)} %bitcast.19, f32[]{:T(128)} %bitcast.18, f32[]{:T(128)} %bitcast.17), kind=kLoop, calls=%fused_computation.189 | loop fusion | flops 786432 | bytes 786448 | tf_op jit(solution)/shard_map/broadcast_in_dim | solution.py:276
  12.9 3.8 %collective-permute-start.7 = (f32[1,16,32,1]{3,2,1,0:T(8,128)}, f32[1,16,32,1]{3,2,1,0:T(8,128)S(1)}, u32[]{:S(2)}, u32[]{:S(2)}) collective-permute-start(f32[1,16,32,1]{3,2,1,0:T(8,128)} %get-tuple-element.206), channel_id=1, source_target_pairs={{8,0},{16,8},{24,16},{0,24},{9,1},{17,9},{25,17},{1,25},{10,2},{18... | collective-permute-start | bytes 6152 | tf_op jit(solution)/shard_map/ppermute | solution.py:30
  17.5 3.8 %collective-permute-start.13 = (f32[1,16,32,1]{3,2,1,0:T(8,128)}, f32[1,16,32,1]{3,2,1,0:T(8,128)S(1)}, u32[]{:S(2)}, u32[]{:S(2)}) collective-permute-start(f32[1,16,32,1]{3,2,1,0:T(8,128)} %get-tuple-element.208), channel_id=1, source_target_pairs={{8,0},{16,8},{24,16},{0,24},{9,1},{17,9},{25,17},{1,25},{10,2},{18... | collective-permute-start | bytes 6152 | tf_op jit(solution)/shard_map/ppermute | solution.py:30
  23.7 2.4 %collective-permute-done.7 = f32[1,16,32,1]{3,2,1,0:T(8,128)S(1)} collective-permute-done((f32[1,16,32,1]{3,2,1,0:T(8,128)}, f32[1,16,32,1]{3,2,1,0:T(8,128)S(1)}, u32[]{:S(2)}, u32[]{:S(2)}) %collective-permute-start.7) | collective-permute-done | bytes 2080 | tf_op jit(solution)/shard_map/ppermute | solution.py:30
  26.6 5.1 %collective-permute-done.6 = f32[1,16,32,1]{3,2,1,0:T(8,128)S(1)} collective-permute-done((f32[1,16,32,1]{3,2,1,0:T(8,128)S(1)}, f32[1,16,32,1]{3,2,1,0:T(8,128)S(1)}, u32[]{:S(2)}, u32[]{:S(2)}) %collective-permute-start.6) | collective-permute-done | bytes 2080 | tf_op jit(solution)/shard_map/ppermute | solution.py:28
  33.3 3.9 %collective-permute-done.13 = f32[1,16,32,1]{3,2,1,0:T(8,128)S(1)} collective-permute-done((f32[1,16,32,1]{3,2,1,0:T(8,128)}, f32[1,16,32,1]{3,2,1,0:T(8,128)S(1)}, u32[]{:S(2)}, u32[]{:S(2)}) %collective-permute-start.13) | collective-permute-done | bytes 2080 | tf_op jit(solution)/shard_map/ppermute | solution.py:30
  38.7 3.0 %collective-permute-done.12 = f32[1,16,32,1]{3,2,1,0:T(8,128)S(1)} collective-permute-done((f32[1,16,32,1]{3,2,1,0:T(8,128)S(1)}, f32[1,16,32,1]{3,2,1,0:T(8,128)S(1)}, u32[]{:S(2)}, u32[]{:S(2)}) %collective-permute-start.12) | collective-permute-done | bytes 2080 | tf_op jit(solution)/shard_map/ppermute | solution.py:28
  58.3 2.8 %collective-permute-done.5 = f32[2,24,4,136]{3,2,1,0:T(4,128)S(1)} collective-permute-done((f32[2,24,4,136]{3,2,1,0:T(4,128)S(1)}, f32[2,24,4,136]{3,2,1,0:T(4,128)S(1)}, u32[]{:S(2)}, u32[]{:S(2)}) %collective-permute-start.5) | collective-permute-done | bytes 104480 | tf_op jit(solution)/shard_map/ppermute | solution.py:30
  61.0 3.0 %collective-permute-done.4 = f32[2,24,4,136]{3,2,1,0:T(4,128)S(1)} collective-permute-done((f32[2,24,4,136]{3,2,1,0:T(4,128)S(1)}, f32[2,24,4,136]{3,2,1,0:T(4,128)S(1)}, u32[]{:S(2)}, u32[]{:S(2)}) %collective-permute-start.4) | collective-permute-done | bytes 104480 | tf_op jit(solution)/shard_map/ppermute | solution.py:28
  73.3 3.9 %all-to-all-start = ((f32[8,1,512]{2,1,0:T(1,128)}), f32[8,1,512]{2,1,0:T(1,128)}, u32[]{:S(2)}, u32[]{:S(2)}) async-start(f32[8,1,512]{2,1,0:T(1,128)} %compare_select_fusion), calls=%async_computation | async-start | bytes 32768 | tf_op jit(solution)/shard_map/all_to_all | solution.py:260
  77.3 2.7 %fusion.126 = (f32[18,34,128]{2,1,0:T(8,128)}, f32[18,34,128]{2,1,0:T(8,128)}, f32[18,34,128]{2,1,0:T(8,128)}, f32[18,34,128]{2,1,0:T(8,128)}) fusion(f32[18,34,130]{2,1,0:T(8,128)S(1)} %pad_multiply_fusion, f32[18,34,129]{2,1,0:T(8,128)} %fusion.27), kind=kLoop, calls=%fused_computation.298 | loop fusion | bytes 2506752 | tf_op jit(solution)/shard_map/slice | solution.py:93
  84.1 2.7 %fusion = f32[128,256]{1,0:T(8,128)S(1)} fusion(f32[4096,128]{0,1:T(8,128)S(1)} %get-tuple-element.216, f32[4096,128]{0,1:T(8,128)S(1)} %get-tuple-element.215, s32[4096]{0:T(1024)S(1)} %copy-done.17), kind=kOutput, calls=%fused_computation.2 | convolution fusion | flops 1612709888 | bytes 4341760 | tf_op jit(solution)/shard_map/while/body/eval_jaxpr/dot_general | solution.py:182
  86.9 3.1 %fusion.104 = (f32[1,16,32,128]{3,2,1,0:T(8,128)S(1)}, f32[16,32,128]{2,1,0:T(8,128)S(1)}, f32[16,32,128]{2,1,0:T(8,128)S(1)}) fusion(f32[16,32,128]{2,1,0:T(8,128)S(1)} %copy-done, f32[4,32,128]{2,1,0:T(8,128)S(1)} %bitcast.119, f32[18,34,128]{2,1,0:T(8,128)S(1)} %copy-done.6, f32[18,34,128]{2,1,0:T(8,128)S(1)} %copy-done.7, ...), kind=kLoop, calls=%fused_computation.213 | loop fusion | flops 1114112 | bytes 4325376 | tf_op jit(solution)/shard_map/broadcast_in_dim | solution.py:282
  92.2 7.1 %collective-permute-done.19 = f32[1,16,32,1]{3,2,1,0:T(8,128)S(1)} collective-permute-done((f32[1,16,32,1]{3,2,1,0:T(8,128)S(1)}, f32[1,16,32,1]{3,2,1,0:T(8,128)S(1)}, u32[]{:S(2)}, u32[]{:S(2)}) %collective-permute-start.19) | collective-permute-done | bytes 2080 | tf_op jit(solution)/shard_map/ppermute | solution.py:30
  99.3 4.6 %collective-permute-done.18 = f32[1,16,32,1]{3,2,1,0:T(8,128)S(1)} collective-permute-done((f32[1,16,32,1]{3,2,1,0:T(8,128)S(1)}, f32[1,16,32,1]{3,2,1,0:T(8,128)S(1)}, u32[]{:S(2)}, u32[]{:S(2)}) %collective-permute-start.18) | collective-permute-done | bytes 2080 | tf_op jit(solution)/shard_map/ppermute | solution.py:28
  114.4 2.4 %collective-permute-start.25 = (f32[1,16,32,1]{3,2,1,0:T(8,128)S(1)}, f32[1,16,32,1]{3,2,1,0:T(8,128)S(1)}, u32[]{:S(2)}, u32[]{:S(2)}) collective-permute-start(f32[1,16,32,1]{3,2,1,0:T(8,128)S(1)} %get-tuple-element.202), channel_id=1, source_target_pairs={{8,0},{16,8},{24,16},{0,24},{9,1},{17,9},{25,17},{1,25},{10,2},{18... | collective-permute-start | bytes 6152 | tf_op jit(solution)/shard_map/ppermute | solution.py:30
  116.9 6.7 %collective-permute-done.25 = f32[1,16,32,1]{3,2,1,0:T(8,128)S(1)} collective-permute-done((f32[1,16,32,1]{3,2,1,0:T(8,128)S(1)}, f32[1,16,32,1]{3,2,1,0:T(8,128)S(1)}, u32[]{:S(2)}, u32[]{:S(2)}) %collective-permute-start.25) | collective-permute-done | bytes 2080 | tf_op jit(solution)/shard_map/ppermute | solution.py:30
  123.6 5.7 %collective-permute-done.24 = f32[1,16,32,1]{3,2,1,0:T(8,128)S(1)} collective-permute-done((f32[1,16,32,1]{3,2,1,0:T(8,128)S(1)}, f32[1,16,32,1]{3,2,1,0:T(8,128)S(1)}, u32[]{:S(2)}, u32[]{:S(2)}) %collective-permute-start.24) | collective-permute-done | bytes 2080 | tf_op jit(solution)/shard_map/ppermute | solution.py:28
  142.3 6.8 %collective-permute-done.31 = f32[1,16,32,1]{3,2,1,0:T(8,128)S(1)} collective-permute-done((f32[1,16,32,1]{3,2,1,0:T(8,128)S(1)}, f32[1,16,32,1]{3,2,1,0:T(8,128)S(1)}, u32[]{:S(2)}, u32[]{:S(2)}) %collective-permute-start.31) | collective-permute-done | bytes 2080 | tf_op jit(solution)/shard_map/ppermute | solution.py:30
  149.1 4.7 %collective-permute-done.30 = f32[1,16,32,1]{3,2,1,0:T(8,128)S(1)} collective-permute-done((f32[1,16,32,1]{3,2,1,0:T(8,128)S(1)}, f32[1,16,32,1]{3,2,1,0:T(8,128)S(1)}, u32[]{:S(2)}, u32[]{:S(2)}) %collective-permute-start.30) | collective-permute-done | bytes 2080 | tf_op jit(solution)/shard_map/ppermute | solution.py:28
  167.7 3.6 %all-to-all-start.1 = ((f32[8,1,512]{2,1,0:T(1,128)}), f32[8,1,512]{2,1,0:T(1,128)S(1)}, u32[]{:S(2)}, u32[]{:S(2)}) async-start(f32[8,1,512]{2,1,0:T(1,128)} %compare_select_fusion.1), calls=%async_computation.1 | async-start | bytes 32768 | tf_op jit(solution)/shard_map/all_to_all | solution.py:291
  171.4 2.3 %fusion.101 = f32[16,16,128]{2,1,0:T(8,128)} fusion(f32[16,16,128]{2,1,0:T(8,128)S(1)} %copy-done.1, f32[16,16,128]{2,1,0:T(8,128)S(1)} %copy-done.10, f32[18,18,128]{2,1,0:T(8,128)S(1)} %copy-done.9, f32[18,18,128]{2,1,0:T(8,128)S(1)} %get-tuple-element.195, f32[18,16,130]{2,1,0:T(8,128)} %get-tuple-element.194, f32[18,16,130]{2,1,0:T(8,128)} %get-tuple-element.193, ...), kind=kLoop, calls=%fused_computation.204 | loop fusion | flops 327680 | bytes 1310720 | tf_op jit(solution)/shard_map/add | solution.py:249
  175.8 2.3 %fusion.4 = f32[64,128]{1,0:T(8,128)S(1)} fusion(f32[4096]{0:T(1024)S(1)} %broadcast_select_fusion, s32[4096]{0:T(1024)S(1)} %copy-done.16, s32[4096]{0:T(1024)S(1)} %copy-done.14), kind=kOutput, calls=%fused_computation.6 | convolution fusion | flops 404226048 | bytes 81920 | tf_op jit(solution)/shard_map/while/body/eval_jaxpr/dot_general | solution.py:182
  (234 shorter events, 82.1 us)
Async XLA Ops:
  1.9 41.5 %collective-permute-start.1 = (f32[2,16,16,4]{3,2,1,0:T(8,128)S(1)}, f32[2,16,16,4]{3,2,1,0:T(8,128)S(1)}, u32[]{:S(2)}, u32[]{:S(2)}) collective-permute-start(f32[2,16,16,4]{3,2,1,0:T(8,128)S(1)} %get-tuple-element.210), channel_id=1, source_target_pairs={{8,0},{16,8},{24,16},{0,24},{9,1},{17,9},{25,17},{1,25},{10,2},{18... | collective-permute-start | bytes 24584 | tf_op jit(solution)/shard_map/ppermute | solution.py:30
  7.0 36.9 %collective-permute-start = (f32[2,16,16,4]{3,2,1,0:T(8,128)S(1)}, f32[2,16,16,4]{3,2,1,0:T(8,128)S(1)}, u32[]{:S(2)}, u32[]{:S(2)}) collective-permute-start(f32[2,16,16,4]{3,2,1,0:T(8,128)S(1)} %get-tuple-element.209), channel_id=1, source_target_pairs={{0,8},{8,16},{16,24},{24,0},{1,9},{9,17},{17,25},{25,1},{2,10},{10... | collective-permute-start | bytes 24584 | tf_op jit(solution)/shard_map/ppermute | solution.py:28
  12.9 13.3 %collective-permute-start.7 = (f32[1,16,32,1]{3,2,1,0:T(8,128)}, f32[1,16,32,1]{3,2,1,0:T(8,128)S(1)}, u32[]{:S(2)}, u32[]{:S(2)}) collective-permute-start(f32[1,16,32,1]{3,2,1,0:T(8,128)} %get-tuple-element.206), channel_id=1, source_target_pairs={{8,0},{16,8},{24,16},{0,24},{9,1},{17,9},{25,17},{1,25},{10,2},{18... | collective-permute-start | bytes 6152 | tf_op jit(solution)/shard_map/ppermute | solution.py:30
  16.7 15.0 %collective-permute-start.6 = (f32[1,16,32,1]{3,2,1,0:T(8,128)S(1)}, f32[1,16,32,1]{3,2,1,0:T(8,128)S(1)}, u32[]{:S(2)}, u32[]{:S(2)}) collective-permute-start(f32[1,16,32,1]{3,2,1,0:T(8,128)S(1)} %get-tuple-element.205), channel_id=1, source_target_pairs={{0,8},{8,16},{16,24},{24,0},{1,9},{9,17},{17,25},{25,1},{2,10},{10... | collective-permute-start | bytes 6152 | tf_op jit(solution)/shard_map/ppermute | solution.py:28
  17.5 19.7 %collective-permute-start.13 = (f32[1,16,32,1]{3,2,1,0:T(8,128)}, f32[1,16,32,1]{3,2,1,0:T(8,128)S(1)}, u32[]{:S(2)}, u32[]{:S(2)}) collective-permute-start(f32[1,16,32,1]{3,2,1,0:T(8,128)} %get-tuple-element.208), channel_id=1, source_target_pairs={{8,0},{16,8},{24,16},{0,24},{9,1},{17,9},{25,17},{1,25},{10,2},{18... | collective-permute-start | bytes 6152 | tf_op jit(solution)/shard_map/ppermute | solution.py:30
  26.1 15.6 %collective-permute-start.12 = (f32[1,16,32,1]{3,2,1,0:T(8,128)S(1)}, f32[1,16,32,1]{3,2,1,0:T(8,128)S(1)}, u32[]{:S(2)}, u32[]{:S(2)}) collective-permute-start(f32[1,16,32,1]{3,2,1,0:T(8,128)S(1)} %get-tuple-element.207), channel_id=1, source_target_pairs={{0,8},{8,16},{16,24},{24,0},{1,9},{9,17},{17,25},{25,1},{2,10},{10... | collective-permute-start | bytes 6152 | tf_op jit(solution)/shard_map/ppermute | solution.py:28
  31.7 14.0 %collective-permute-start.9 = (f32[1,1,32,130]{3,2,1,0:T(8,128)S(1)}, f32[1,1,32,130]{3,2,1,0:T(8,128)S(1)}, u32[]{:S(2)}, u32[]{:S(2)}) collective-permute-start(f32[1,1,32,130]{3,2,1,0:T(8,128)S(1)} %get-tuple-element.138), channel_id=1, source_target_pairs={{4,0},{0,4},{5,1},{1,5},{6,2},{2,6},{7,3},{3,7},{12,8},{8,12},{13,... | collective-permute-start | bytes 49928 | tf_op jit(solution)/shard_map/ppermute | solution.py:30
  37.2 9.0 %collective-permute-start.8 = (f32[1,1,32,130]{3,2,1,0:T(8,128)S(1)}, f32[1,1,32,130]{3,2,1,0:T(8,128)S(1)}, u32[]{:S(2)}, u32[]{:S(2)}) collective-permute-start(f32[1,1,32,130]{3,2,1,0:T(8,128)S(1)} %get-tuple-element.137), channel_id=1, source_target_pairs={{0,4},{4,0},{1,5},{5,1},{2,6},{6,2},{3,7},{7,3},{8,12},{12,8},{9,1... | collective-permute-start | bytes 49928 | tf_op jit(solution)/shard_map/ppermute | solution.py:28
  41.8 4.6 %collective-permute-start.15 = (f32[1,1,32,130]{3,2,1,0:T(8,128)S(1)}, f32[1,1,32,130]{3,2,1,0:T(8,128)S(1)}, u32[]{:S(2)}, u32[]{:S(2)}) collective-permute-start(f32[1,1,32,130]{3,2,1,0:T(8,128)S(1)} %get-tuple-element.140), channel_id=1, source_target_pairs={{4,0},{0,4},{5,1},{1,5},{6,2},{2,6},{7,3},{3,7},{12,8},{8,12},{13,... | collective-permute-start | bytes 49928 | tf_op jit(solution)/shard_map/ppermute | solution.py:30
  43.4 4.3 %collective-permute-start.14 = (f32[1,1,32,130]{3,2,1,0:T(8,128)S(1)}, f32[1,1,32,130]{3,2,1,0:T(8,128)S(1)}, u32[]{:S(2)}, u32[]{:S(2)}) collective-permute-start(f32[1,1,32,130]{3,2,1,0:T(8,128)S(1)} %get-tuple-element.139), channel_id=1, source_target_pairs={{0,4},{4,0},{1,5},{5,1},{2,6},{6,2},{3,7},{7,3},{8,12},{12,8},{9,1... | collective-permute-start | bytes 49928 | tf_op jit(solution)/shard_map/ppermute | solution.py:28
  44.1 12.2 %collective-permute-start.3 = (f32[2,4,16,136]{3,2,1,0:T(8,128)S(1)}, f32[2,4,16,136]{3,2,1,0:T(8,128)S(1)}, u32[]{:S(2)}, u32[]{:S(2)}) collective-permute-start(f32[2,4,16,136]{3,2,1,0:T(8,128)S(1)} %get-tuple-element.142), channel_id=1, source_target_pairs={{4,0},{0,4},{5,1},{1,5},{6,2},{2,6},{7,3},{3,7},{12,8},{8,12},{13,... | collective-permute-start | bytes 208904 | tf_op jit(solution)/shard_map/ppermute | solution.py:30
  45.7 10.6 %collective-permute-start.2 = (f32[2,4,16,136]{3,2,1,0:T(8,128)S(1)}, f32[2,4,16,136]{3,2,1,0:T(8,128)S(1)}, u32[]{:S(2)}, u32[]{:S(2)}) collective-permute-start(f32[2,4,16,136]{3,2,1,0:T(8,128)S(1)} %get-tuple-element.141), channel_id=1, source_target_pairs={{0,4},{4,0},{1,5},{5,1},{2,6},{6,2},{3,7},{7,3},{8,12},{12,8},{9,1... | collective-permute-start | bytes 208904 | tf_op jit(solution)/shard_map/ppermute | solution.py:28
  56.6 4.4 %collective-permute-start.5 = (f32[2,24,4,136]{3,2,1,0:T(4,128)S(1)}, f32[2,24,4,136]{3,2,1,0:T(4,128)S(1)}, u32[]{:S(2)}, u32[]{:S(2)}) collective-permute-start(f32[2,24,4,136]{3,2,1,0:T(4,128)S(1)} %get-tuple-element.120), channel_id=1, source_target_pairs={{1,0},{2,1},{3,2},{0,3},{5,4},{6,5},{7,6},{4,7},{9,8},{10,9},{11,1... | collective-permute-start | bytes 313352 | tf_op jit(solution)/shard_map/ppermute | solution.py:30
  56.8 7.3 %collective-permute-start.4 = (f32[2,24,4,136]{3,2,1,0:T(4,128)S(1)}, f32[2,24,4,136]{3,2,1,0:T(4,128)S(1)}, u32[]{:S(2)}, u32[]{:S(2)}) collective-permute-start(f32[2,24,4,136]{3,2,1,0:T(4,128)S(1)} %get-tuple-element.119), channel_id=1, source_target_pairs={{0,1},{1,2},{2,3},{3,0},{4,5},{5,6},{6,7},{7,4},{8,9},{9,10},{10,1... | collective-permute-start | bytes 313352 | tf_op jit(solution)/shard_map/ppermute | solution.py:28
  73.3 8.7 %all-to-all-start = ((f32[8,1,512]{2,1,0:T(1,128)}), f32[8,1,512]{2,1,0:T(1,128)}, u32[]{:S(2)}, u32[]{:S(2)}) async-start(f32[8,1,512]{2,1,0:T(1,128)} %compare_select_fusion), calls=%async_computation | async-start | bytes 32768 | tf_op jit(solution)/shard_map/all_to_all | solution.py:260
  90.1 9.2 %collective-permute-start.19 = (f32[1,16,32,1]{3,2,1,0:T(8,128)S(1)}, f32[1,16,32,1]{3,2,1,0:T(8,128)S(1)}, u32[]{:S(2)}, u32[]{:S(2)}) collective-permute-start(f32[1,16,32,1]{3,2,1,0:T(8,128)S(1)} %get-tuple-element.204), channel_id=1, source_target_pairs={{8,0},{16,8},{24,16},{0,24},{9,1},{17,9},{25,17},{1,25},{10,2},{18... | collective-permute-start | bytes 6152 | tf_op jit(solution)/shard_map/ppermute | solution.py:30
  91.8 12.1 %collective-permute-start.18 = (f32[1,16,32,1]{3,2,1,0:T(8,128)S(1)}, f32[1,16,32,1]{3,2,1,0:T(8,128)S(1)}, u32[]{:S(2)}, u32[]{:S(2)}) collective-permute-start(f32[1,16,32,1]{3,2,1,0:T(8,128)S(1)} %get-tuple-element.203), channel_id=1, source_target_pairs={{0,8},{8,16},{16,24},{24,0},{1,9},{9,17},{17,25},{25,1},{2,10},{10... | collective-permute-start | bytes 6152 | tf_op jit(solution)/shard_map/ppermute | solution.py:28
  104.0 4.0 %collective-permute-start.21 = (f32[1,1,32,130]{3,2,1,0:T(8,128)S(1)}, f32[1,1,32,130]{3,2,1,0:T(8,128)S(1)}, u32[]{:S(2)}, u32[]{:S(2)}) collective-permute-start(f32[1,1,32,130]{3,2,1,0:T(8,128)S(1)} %get-tuple-element.136), channel_id=1, source_target_pairs={{4,0},{0,4},{5,1},{1,5},{6,2},{2,6},{7,3},{3,7},{12,8},{8,12},{13,... | collective-permute-start | bytes 49928 | tf_op jit(solution)/shard_map/ppermute | solution.py:30
  114.4 9.1 %collective-permute-start.25 = (f32[1,16,32,1]{3,2,1,0:T(8,128)S(1)}, f32[1,16,32,1]{3,2,1,0:T(8,128)S(1)}, u32[]{:S(2)}, u32[]{:S(2)}) collective-permute-start(f32[1,16,32,1]{3,2,1,0:T(8,128)S(1)} %get-tuple-element.202), channel_id=1, source_target_pairs={{8,0},{16,8},{24,16},{0,24},{9,1},{17,9},{25,17},{1,25},{10,2},{18... | collective-permute-start | bytes 6152 | tf_op jit(solution)/shard_map/ppermute | solution.py:30
  116.8 12.5 %collective-permute-start.24 = (f32[1,16,32,1]{3,2,1,0:T(8,128)S(1)}, f32[1,16,32,1]{3,2,1,0:T(8,128)S(1)}, u32[]{:S(2)}, u32[]{:S(2)}) collective-permute-start(f32[1,16,32,1]{3,2,1,0:T(8,128)S(1)} %get-tuple-element.201), channel_id=1, source_target_pairs={{0,8},{8,16},{16,24},{24,0},{1,9},{9,17},{17,25},{25,1},{2,10},{10... | collective-permute-start | bytes 6152 | tf_op jit(solution)/shard_map/ppermute | solution.py:28
  129.4 4.0 %collective-permute-start.27 = (f32[1,1,32,130]{3,2,1,0:T(8,128)S(1)}, f32[1,1,32,130]{3,2,1,0:T(8,128)S(1)}, u32[]{:S(2)}, u32[]{:S(2)}) collective-permute-start(f32[1,1,32,130]{3,2,1,0:T(8,128)S(1)} %get-tuple-element.134), channel_id=1, source_target_pairs={{4,0},{0,4},{5,1},{1,5},{6,2},{2,6},{7,3},{3,7},{12,8},{8,12},{13,... | collective-permute-start | bytes 49928 | tf_op jit(solution)/shard_map/ppermute | solution.py:30
  140.1 9.0 %collective-permute-start.31 = (f32[1,16,32,1]{3,2,1,0:T(8,128)S(1)}, f32[1,16,32,1]{3,2,1,0:T(8,128)S(1)}, u32[]{:S(2)}, u32[]{:S(2)}) collective-permute-start(f32[1,16,32,1]{3,2,1,0:T(8,128)S(1)} %get-tuple-element.200), channel_id=1, source_target_pairs={{8,0},{16,8},{24,16},{0,24},{9,1},{17,9},{25,17},{1,25},{10,2},{18... | collective-permute-start | bytes 6152 | tf_op jit(solution)/shard_map/ppermute | solution.py:30
  141.9 11.9 %collective-permute-start.30 = (f32[1,16,32,1]{3,2,1,0:T(8,128)S(1)}, f32[1,16,32,1]{3,2,1,0:T(8,128)S(1)}, u32[]{:S(2)}, u32[]{:S(2)}) collective-permute-start(f32[1,16,32,1]{3,2,1,0:T(8,128)S(1)} %get-tuple-element.199), channel_id=1, source_target_pairs={{0,8},{8,16},{16,24},{24,0},{1,9},{9,17},{17,25},{25,1},{2,10},{10... | collective-permute-start | bytes 6152 | tf_op jit(solution)/shard_map/ppermute | solution.py:28
  167.7 8.0 %all-to-all-start.1 = ((f32[8,1,512]{2,1,0:T(1,128)}), f32[8,1,512]{2,1,0:T(1,128)S(1)}, u32[]{:S(2)}, u32[]{:S(2)}) async-start(f32[8,1,512]{2,1,0:T(1,128)} %compare_select_fusion.1), calls=%async_computation.1 | async-start | bytes 32768 | tf_op jit(solution)/shard_map/all_to_all | solution.py:291
  (40 other events, 345.6 us)
where the time goes:
time: 180 us; the launch traced here: 179 us
  waiting for transfers between devices  73.9 us (41%)
  starting transfers between devices  45.6 us (25%)
  other arithmetic  33.6 us (19%)
  local copies, waits for them, and re-layouts  15.7 us (9%)
  matrix products  8.61 us (5%)
    ppermute x18, waiting for transfers between devices, with_halo(): lax.ppermute(tail, axis, [(i, (i + 1) % count) for i in range(count)])  36.2 us
    ppermute x18, waiting for transfers between devices, with_halo(): lax.ppermute(head, axis, [((i + 1) % count, i) for i in range(count)])  33.5 us
    ppermute x18, starting transfers between devices, with_halo(): lax.ppermute(head, axis, [((i + 1) % count, i) for i in range(count)])  27.4 us
    ppermute x18, starting transfers between devices, with_halo(): lax.ppermute(tail, axis, [(i, (i + 1) % count) for i in range(count)])  10.7 us
    dot_general x2, matrix products, scatter_one_block(): lax.dot_general(row_hot, weighted, (((0,), (0,)), ((), ())), precision=la...  5.03 us
    all_to_all x1, starting transfers between devices, per_device(): lax.all_to_all(sent_vals, ('gx', 'gy'), split_axis=0, concat_axis=0, tile...  3.94 us
    broadcast_in_dim x1, other arithmetic, per_device(): conduct[None]  3.62 us
  transfers between devices with their start and end apart: 38, of which 28 were waited for; matrix products, arithmetic and copies ran while one was open for 14% of the time, Pallas kernels for 0%

commit v1 on v0

v1 whole, which is shorter than its diff:
```python
import functools

import jax
import jax.numpy as jnp
from jax import lax
from jax.experimental import pallas as pl
from jax.experimental.pallas import tpu as pltpu
from jax.sharding import PartitionSpec as P

LABELS = 4
SWEEPS_H = 3
SWEEPS_T = 4

time_step = 0.1
intra_cond = 0.25
extra_cond = 0.5
penalty = 2.0
cheb_low = 0.1
cheb_high = 2.0

MESH = pl.DeviceIdType.MESH
F32 = jnp.float32
BF16 = jnp.bfloat16


def cheb_coeffs(sweeps):
    centre = 0.5 * (cheb_high + cheb_low)
    half_width = 0.5 * (cheb_high - cheb_low)
    scaled = centre / half_width
    coeffs = [(0.0, 1.0 / centre)]
    rho_old = 1.0 / scaled
    for number in range(1, sweeps):
        rho_new = 1.0 / (2.0 * scaled - rho_old)
        coeffs.append((rho_new * rho_old, 2.0 * rho_new / half_width))
        rho_old = rho_new
    return coeffs


def harmonic(a, b):
    return 2.0 * a * b / (a + b)


def two_terms(values):
    high = values.astype(BF16)
    return high, (values - high.astype(F32)).astype(BF16)


class Grid:
    def __init__(self, shape, stage, landing, sends, recvs, ypad, place):
        self.shape = shape
        self.stage = stage
        self.landing = landing
        self.sends = sends
        self.recvs = recvs
        self.ypad = ypad
        self.place = place

    def clear_ends(self):
        for axis, (_, low, high) in enumerate(self.place):
            for side, (_, present) in enumerate((low, high)):
                if present is None:
                    continue

                @pl.when(jnp.logical_not(present))
                def _(axis=axis, side=side):
                    ref = self.landing[axis]
                    ref[side] = jnp.zeros(ref.shape[1:], F32)

    def pack(self, slot, field):
        nx, ny, nz = self.shape
        xs, ys, zs = self.stage
        xs[0, slot] = field[0]
        xs[1, slot] = field[nx - 1]
        ys[0, slot] = field[:, 0:1, :]
        ys[1, slot] = field[:, ny - 1 : ny, :]
        turned = jnp.transpose(field.reshape(nx * ny, nz))
        zs[0, slot] = turned[0:1, :]
        zs[1, slot] = turned[nz - 1 : nz, :]

    def copies(self, turn, first, count):
        for axis, (name, low, high) in enumerate(self.place):
            for side, there in enumerate((low, high)):
                back = (high, low)[side]
                yield (
                    pltpu.make_async_remote_copy(
                        src_ref=self.stage[axis].at[side, pl.ds(first, count)],
                        dst_ref=self.landing[axis].at[1 - side, pl.ds(first, count)],
                        send_sem=self.sends.at[turn, axis, side],
                        recv_sem=self.recvs.at[turn, axis, 1 - side],
                        device_id={name: there[0]},
                        device_id_type=MESH,
                    ),
                    there[1],
                    back[1],
                )

    def send(self, turn, first, count):
        for copy, out, _ in self.copies(turn, first, count):
            if out is None:
                copy.start()
            else:
                pl.when(out)(copy.start)

    def wait(self, turn, first, count):
        for copy, _, back in self.copies(turn, first, count):
            if back is None:
                copy.wait_recv()
            else:
                pl.when(back)(copy.wait_recv)

    def finish(self, turn, first, count):
        for copy, out, _ in self.copies(turn, first, count):
            if out is None:
                copy.wait_send()
            else:
                pl.when(out)(copy.wait_send)

    def around(self, slot, field):
        nx, ny, nz = self.shape
        rx, ry, rz = self.landing
        below_x = jnp.concatenate([rx[0, slot][None], field[:-1]], axis=0)
        above_x = jnp.concatenate([field[1:], rx[1, slot][None]], axis=0)
        self.ypad[:, 8 : 8 + ny, :] = field
        self.ypad[:, 7:8, :] = ry[0, slot]
        self.ypad[:, 8 + ny : 9 + ny, :] = ry[1, slot]
        below_y = self.ypad[:, 7 : 7 + ny, :]
        above_y = self.ypad[:, 9 : 9 + ny, :]
        depth = lax.broadcasted_iota(jnp.int32, (nz, nx * ny), 0)
        ends = jnp.transpose(jnp.where(depth == 0, rz[0, slot], rz[1, slot]))
        flat = field.reshape(nx * ny, nz)
        lanes = lax.broadcasted_iota(jnp.int32, (nx * ny, nz), 1)
        below_z = jnp.where(lanes == 0, ends, pltpu.roll(flat, 1, 1)).reshape(nx, ny, nz)
        above_z = jnp.where(lanes == nz - 1, ends, pltpu.roll(flat, nz - 1, 1)).reshape(nx, ny, nz)
        return below_x, above_x, below_y, above_y, below_z, above_z


def spots(node_ref, count_ref, peer, rows, width):
    index = node_ref[pl.ds(peer, 1), :]
    cap = index.shape[1]
    slot_ids = lax.broadcasted_iota(jnp.int32, (1, cap), 1)
    index = jnp.where(slot_ids < count_ref[peer], index, -1)
    row_ids = lax.broadcasted_iota(jnp.int32, (rows, cap), 0)
    col_ids = lax.broadcasted_iota(jnp.int32, (width, cap), 0)
    row_hot = jnp.where(row_ids == lax.shift_right_arithmetic(index, 7), 1.0, 0.0).astype(BF16)
    return row_hot, col_ids == (index & (width - 1))


def turned_table(layer, rows, width):
    high, low = two_terms(jnp.transpose(layer.reshape(rows, width)))
    return jnp.concatenate([high, low], axis=1)


def pick(table, row_hot, col_hot):
    chosen = jnp.dot(
        table, jnp.concatenate([row_hot, row_hot], axis=0), preferred_element_type=F32
    )
    return jnp.sum(jnp.where(col_hot, chosen, 0.0), axis=0, keepdims=True)


def place_at(values, row_hot, col_hot):
    high = values.astype(BF16).astype(F32)
    low = values - high
    columns = jnp.concatenate(
        [jnp.where(col_hot, high, 0.0).astype(BF16), jnp.where(col_hot, low, 0.0).astype(BF16)],
        axis=0,
    )
    return lax.dot_general(
        row_hot, columns, (((1,), (1,)), ((), ())), preferred_element_type=F32
    )


def kernel(
    sizes,
    states,
    membrane,
    phi_heart,
    ion_params,
    torso_phi,
    tissue_scale,
    labels,
    cond_table,
    send_node,
    send_count,
    recv_voxel,
    recv_count,
    new_membrane,
    heart_phi,
    torso_out,
    hsx, hsy, hsz, hrx, hry, hrz, hypad, hsend, hrecv,
    tsx, tsy, tsz, trx, try_, trz, typad, tsend, trecv,
    sent, arrived, returned, came,
    out_sem, in_sem, back_sem, home_sem,
    update_h, source_h, current_h, gains, update_t, right_t, weight_t, flux_h,
):
    n_grp, n_gx, n_gy = sizes
    peers = n_gx * n_gy
    unroll = peers <= 8
    g = lax.axis_index("grp")
    i = lax.axis_index("gx")
    j = lax.axis_index("gy")
    me = i * n_gy + j
    hshape = membrane.shape
    tshape = torso_phi.shape
    place = (
        ("gx", (lax.rem(i + n_gx - 1, n_gx), None), (lax.rem(i + 1, n_gx), None)),
        ("gy", (jnp.maximum(j - 1, 0), j > 0), (jnp.minimum(j + 1, n_gy - 1), j < n_gy - 1)),
        ("grp", (jnp.maximum(g - 1, 0), g > 0), (jnp.minimum(g + 1, n_grp - 1), g < n_grp - 1)),
    )
    heart = Grid(hshape, (hsx, hsy, hsz), (hrx, hry, hrz), hsend, hrecv, hypad, place)
    torso = Grid(tshape, (tsx, tsy, tsz), (trx, try_, trz), tsend, trecv, typad, place)

    heart.clear_ends()
    torso.clear_ends()

    def peer_at(step):
        other = lax.rem(me + step, peers)
        return other, {"gx": other // n_gy, "gy": lax.rem(other, n_gy)}

    barrier = pltpu.get_barrier_semaphore()

    def greet(step, carry):
        pl.semaphore_signal(barrier, inc=1, device_id=peer_at(step)[1], device_id_type=MESH)
        return carry

    lax.fori_loop(1, peers, greet, 0, unroll=unroll)
    _, low_z, high_z = place[2]
    for there, present in (low_z, high_z):

        @pl.when(present)
        def _(there=there):
            pl.semaphore_signal(barrier, inc=1, device_id={"grp": there}, device_id_type=MESH)

    heart.pack(0, membrane[...])
    heart.pack(1, phi_heart[...])
    names = labels[...]
    table = jnp.where(names == 0, cond_table[0], 0.0)
    for number in range(1, LABELS):
        table = jnp.where(names == number, cond_table[number], table)
    conduct = tissue_scale[...] * table
    torso.pack(0, conduct)
    torso.pack(1, torso_phi[...])

    pl.semaphore_wait(
        barrier, peers - 1 + (g > 0).astype(jnp.int32) + (g < n_grp - 1).astype(jnp.int32)
    )
    heart.send(0, 0, 2)
    torso.send(0, 0, 2)

    voltage = membrane[...]
    current = jnp.zeros(hshape, F32)
    for state in range(states.shape[0]):
        line = jnp.zeros((1, 1, hshape[2]), F32)
        half_slope = 0.5 / (line + ion_params[1, state])
        decay = jnp.exp(line - time_step * ion_params[2, state])
        steady = 0.5 + 0.5 * jnp.tanh((voltage - ion_params[0, state]) * half_slope)
        gate = steady + (states[state].astype(F32) - steady) * decay
        current = current + ion_params[3, state] * gate * (voltage - ion_params[4, state])
    current_h[...] = current

    ny = lax.broadcasted_iota(jnp.int32, hshape, 1) + j * hshape[1]
    nz = lax.broadcasted_iota(jnp.int32, hshape, 2) + g * hshape[2]
    diag = (
        6.0
        - jnp.where(ny == 0, 1.0, 0.0)
        - jnp.where(ny == hshape[1] * n_gy - 1, 1.0, 0.0)
        - jnp.where(nz == 0, 1.0, 0.0)
        - jnp.where(nz == hshape[2] * n_grp - 1, 1.0, 0.0)
    )
    inverse = 1.0 / diag

    def total_of(parts):
        return ((parts[0] + parts[1]) + (parts[2] + parts[3])) + (parts[4] + parts[5])

    heart.wait(0, 0, 2)
    lap_mem = diag * voltage - total_of(heart.around(0, voltage))
    source_h[...] = lap_mem
    base = (-intra_cond / (intra_cond + extra_cond)) * lap_mem * inverse
    iterate = phi_heart[...]
    update = None
    for number, (carry_coef, resid_coef) in enumerate(cheb_coeffs(SWEEPS_H)):
        if number > 0:
            heart.wait(number, number + 1, 1)
        around = total_of(heart.around(number + 1, iterate))
        residue = base - iterate + around * inverse
        update = resid_coef * residue if update is None else carry_coef * update + resid_coef * residue
        iterate = iterate + update
        heart.pack(number + 2, iterate)
        heart.send(number + 1, number + 2, 1)
        if number == 0:
            rows = tshape[0] // 4 * tshape[1]

            def weigh(peer, carry):
                row_hot, col_hot = spots(recv_voxel, recv_count, peer, rows, tshape[2])
                ones = jnp.where(col_hot, 1.0, 0.0).astype(BF16)
                return carry + lax.dot_general(
                    row_hot, ones, (((1,), (1,)), ((), ())), preferred_element_type=F32
                )

            weight_t[...] = penalty * lax.fori_loop(
                0, peers, weigh, jnp.zeros((rows, tshape[2]), F32), unroll=unroll
            )
    phi_new = iterate

    layer_h = hshape[0] // 4
    rows_h = layer_h * hshape[1]
    table_h = turned_table(phi_new[:layer_h], rows_h, hshape[2])

    def patch(step, source, target, sends, recvs):
        other, where = peer_at(step)
        return pltpu.make_async_remote_copy(
            src_ref=source.at[other],
            dst_ref=target.at[me],
            send_sem=sends.at[other],
            recv_sem=recvs.at[me],
            device_id=where,
            device_id_type=MESH,
        )

    def landed(step, source, target, sends, recvs):
        other, where = peer_at(step)
        return pltpu.make_async_remote_copy(
            src_ref=source.at[other],
            dst_ref=target.at[other],
            send_sem=sends.at[other],
            recv_sem=recvs.at[other],
            device_id=where,
            device_id_type=MESH,
        )

    def give(step, carry):
        other, _ = peer_at(step)
        row_hot, col_hot = spots(send_node, send_count, other, rows_h, hshape[2])
        sent[other] = pick(table_h, row_hot, col_hot)
        patch(step, sent, arrived, out_sem, in_sem).start()
        return carry

    lax.fori_loop(1, peers, give, 0, unroll=unroll)
    row_hot, col_hot = spots(send_node, send_count, me, rows_h, hshape[2])
    arrived[me] = pick(table_h, row_hot, col_hot)

    heart.wait(SWEEPS_H, SWEEPS_H + 1, 1)
    lap_phi = diag * phi_new - total_of(heart.around(SWEEPS_H + 1, phi_new))
    new_membrane[...] = voltage + time_step * (
        -intra_cond * (source_h[...] + lap_phi) - current_h[...]
    )
    update_h[...] = phi_new

    torso.wait(0, 0, 2)
    layer = tshape[0] // 4
    rows = layer * tshape[1]
    faces = [harmonic(conduct, other) for other in torso.around(0, conduct)]
    weight = weight_t[...].reshape(layer, tshape[1], tshape[2])
    total = total_of(faces)
    total = jnp.concatenate([total[:layer] + weight, total[layer:]], axis=0)
    scale = 1.0 / total
    for number in range(6):
        gains[number] = faces[number] * scale
    right_t[...] = penalty * scale[:layer]
    iterate = torso_phi[...]
    update_t[...] = -iterate + total_of(
        [gains[n] * other for n, other in enumerate(torso.around(1, iterate))]
    )

    def gather_right(step, carry):
        other, _ = peer_at(step)
        landed(step, sent, arrived, out_sem, in_sem).wait_recv()
        row_hot, col_hot = spots(recv_voxel, recv_count, other, rows, tshape[2])
        return carry + place_at(arrived[other], row_hot, col_hot)

    row_hot, col_hot = spots(recv_voxel, recv_count, me, rows, tshape[2])
    summed = place_at(arrived[me], row_hot, col_hot)
    summed = lax.fori_loop(1, peers, gather_right, summed, unroll=unroll)
    summed = summed[:, : tshape[2]] + summed[:, tshape[2] :]
    right = summed.reshape(layer, tshape[1], tshape[2]) * right_t[...]
    right_t[...] = right

    coeffs = cheb_coeffs(SWEEPS_T)
    update = update_t[...]
    update = coeffs[0][1] * jnp.concatenate([update[:layer] + right, update[layer:]], axis=0)
    iterate = iterate + update
    for number in range(1, SWEEPS_T):
        torso.pack(number + 1, iterate)
        torso.send(number, number + 1, 1)
        torso.wait(number, number + 1, 1)
        residue = -iterate + total_of(
            [gains[n] * other for n, other in enumerate(torso.around(number + 1, iterate))]
        )
        residue = jnp.concatenate([residue[:layer] + right_t[...], residue[layer:]], axis=0)
        update = coeffs[number][0] * update + coeffs[number][1] * residue
        iterate = iterate + update
    table_t = turned_table(iterate[:layer], rows, tshape[2])

    def give_back(step, carry):
        other, _ = peer_at(step)
        row_hot, col_hot = spots(recv_voxel, recv_count, other, rows, tshape[2])
        returned[other] = penalty * (arrived[other] - pick(table_t, row_hot, col_hot))
        patch(step, returned, came, back_sem, home_sem).start()
        return carry

    lax.fori_loop(1, peers, give_back, 0, unroll=unroll)
    row_hot, col_hot = spots(recv_voxel, recv_count, me, rows, tshape[2])
    came[me] = penalty * (arrived[me] - pick(table_t, row_hot, col_hot))
    torso_out[...] = iterate
    phi_new = update_h[...]
    heart_phi[...] = phi_new

    heart.finish(0, 0, 2)
    torso.finish(0, 0, 2)
    for number in range(1, SWEEPS_H + 1):
        heart.finish(number, number + 1, 1)
    for number in range(1, SWEEPS_T):
        torso.finish(number, number + 1, 1)

    def take_back(step, carry):
        other, _ = peer_at(step)
        landed(step, returned, came, back_sem, home_sem).wait_recv()
        row_hot, col_hot = spots(send_node, send_count, other, rows_h, hshape[2])
        return carry + place_at(came[other], row_hot, col_hot)

    row_hot, col_hot = spots(send_node, send_count, me, rows_h, hshape[2])
    flux = place_at(came[me], row_hot, col_hot)
    flux = lax.fori_loop(1, peers, take_back, flux, unroll=unroll)
    flux = (flux[:, : hshape[2]] + flux[:, hshape[2] :]).reshape(layer_h, hshape[1], hshape[2])
    heart_phi[0:layer_h] = phi_new[:layer_h] - flux * (
        inverse[:layer_h] * (1.0 / (intra_cond + extra_cond))
    )

    def settle(step, carry):
        landed(step, sent, arrived, out_sem, in_sem).wait_send()
        landed(step, returned, came, back_sem, home_sem).wait_send()
        return carry

    lax.fori_loop(1, peers, settle, 0, unroll=unroll)


def per_device(sizes, *args):
    (
        states,
        membrane,
        phi_heart,
        ion_params,
        torso_phi,
        tissue_scale,
        labels,
        cond_table,
        send_node,
        send_count,
        recv_voxel,
        recv_count,
    ) = args
    peers, cap = send_node.shape[-2:]
    hx, hy, hz = membrane.shape
    tx, ty, tz = torso_phi.shape
    vmem = pl.BlockSpec(memory_space=pltpu.VMEM)
    smem = pl.BlockSpec(memory_space=pltpu.SMEM)

    def grid_scratch(shape, slots, turns):
        nx, ny, nz = shape
        faces = [
            pltpu.VMEM((2, slots, ny, nz), F32),
            pltpu.VMEM((2, slots, nx, 1, nz), F32),
            pltpu.VMEM((2, slots, 1, nx * ny), F32),
        ]
        return (
            faces
            + faces
            + [
                pltpu.VMEM((nx, ny + 16, nz), F32),
                pltpu.SemaphoreType.DMA((turns, 3, 2)),
                pltpu.SemaphoreType.DMA((turns, 3, 2)),
            ]
        )

    patches = [pltpu.VMEM((peers, 1, cap), F32)] * 4
    signals = [pltpu.SemaphoreType.DMA((peers,))] * 4
    block = pltpu.VMEM((hx, hy, hz), F32)
    work = [
        block,
        block,
        block,
        pltpu.VMEM((6, tx, ty, tz), F32),
        pltpu.VMEM((tx, ty, tz), F32),
        pltpu.VMEM((tx // 4, ty, tz), F32),
        pltpu.VMEM((tx // 4 * ty, tz), F32),
        pltpu.VMEM((hx // 4 * hy, hz), F32),
    ]
    return pl.pallas_call(
        functools.partial(kernel, sizes),
        out_shape=(
            jax.ShapeDtypeStruct(membrane.shape, F32),
            jax.ShapeDtypeStruct(membrane.shape, F32),
            jax.ShapeDtypeStruct(torso_phi.shape, F32),
        ),
        in_specs=[vmem, vmem, vmem, smem, vmem, vmem, vmem, smem, vmem, smem, vmem, smem],
        out_specs=(vmem, vmem, vmem),
        scratch_shapes=grid_scratch(membrane.shape, SWEEPS_H + 2, SWEEPS_H + 1)
        + grid_scratch(torso_phi.shape, SWEEPS_T + 1, SWEEPS_T)
        + patches
        + signals
        + work,
        compiler_params=pltpu.CompilerParams(
            collective_id=0, has_side_effects=True, vmem_limit_bytes=48 * 1024 * 1024
        ),
    )(
        states,
        membrane,
        phi_heart,
        ion_params,
        torso_phi,
        tissue_scale,
        labels,
        cond_table,
        send_node.reshape(peers, cap),
        send_count.reshape(peers),
        recv_voxel.reshape(peers, cap),
        recv_count.reshape(peers),
    )


def solution(mesh):
    sizes = (mesh.shape["grp"], mesh.shape["gx"], mesh.shape["gy"])
    placed = (
        P(None, "gx", "gy", "grp"),
        P("gx", "gy", "grp"),
        P("gx", "gy", "grp"),
        P(),
        P("gx", "gy", "grp"),
        P("gx", "gy", "grp"),
        P("gx", "gy", "grp"),
        P(),
        P("grp", "gx", "gy", None, None),
        P("grp", "gx", "gy", None),
        P("grp", "gx", "gy", None, None),
        P("grp", "gx", "gy", None),
    )
    return jax.shard_map(
        functools.partial(per_device, sizes),
        mesh=mesh,
        in_specs=placed,
        out_specs=(P("gx", "gy", "grp"), P("gx", "gy", "grp"), P("gx", "gy", "grp")),
        check_vma=False,
    )
```

time: 180 us -> 48.2 us (0.27)
  waiting for transfers between devices: 73.9 us -> 0 us
  starting transfers between devices: 45.6 us -> 0 us
  Pallas kernels: 0 us -> 37.1 us
  other arithmetic: 33.6 us -> 0 us
  matrix products: 8.61 us -> 0 us
  local copies, waits for them, and re-layouts: 15.7 us -> 9.91 us
    ppermute x36 -> x0, waiting for transfers between devices: 69.7 us -> none  [the longest x18 36.2 us: with_halo(): lax.ppermute(tail, axis, [(i, (i + 1) % count) for i in range(count)])]
    ppermute x36 -> x0, starting transfers between devices: 38 us -> none  [the longest x18 27.4 us: with_halo(): lax.ppermute(head, axis, [((i + 1) % count, i) for i in range(count)])]
    pallas_call x0 -> x1, Pallas kernels: none -> 37.1 us  [per_device(): pl.pallas_call(functools.partial(kernel, sizes), out_shape=(jax.ShapeDtyp...]
    slice x38 -> x0, local copies, waits for them, and re-layouts: 14.6 us -> none  [the longest x1 2.69 us: face_total(): return summed + (face_z[:, :, :-2] + face_z[:, :, 1:-1])[1:-1, 1:-1, :]]
    unnamed x56 -> x27, local copies, waits for them, and re-layouts: 1.07 us -> 9.91 us
    dot_general x4 -> x0, matrix products: 8.61 us -> none  [the longest x2 5.03 us: scatter_one_block(): lax.dot_general(row_hot, weighted, (((0,), (0,)), ((), ())), precision=la...]
    all_to_all x2 -> x0, starting transfers between devices: 7.53 us -> none  [the longest x1 3.94 us: per_device(): lax.all_to_all(sent_vals, ('gx', 'gy'), split_axis=0, concat_axis=0, tile...]
    mul x28 -> x0, other arithmetic: 7.1 us -> none  [the longest x8 2.87 us: flux_sum(): along_z = face_z[:, :, :-1] * (values[:, :, 1:] - values[:, :, :-1])]
  transfers between devices with their start and end apart: 38 -> 0, of which waited for: 28 -> 0; matrix products, arithmetic and copies ran while one was open for 14% -> 0% of each run, Pallas kernels for 0% -> 0%
where the time goes in v1:
time: 48.2 us; the launch traced here: 47.7 us
  Pallas kernels  37.1 us (77%)
  local copies, waits for them, and re-layouts  9.91 us (21%)
  between operations  0.69 us (1%)
    pallas_call x1, Pallas kernels, per_device(): pl.pallas_call(functools.partial(kernel, sizes), out_shape=(jax.ShapeDtyp...  37.1 us
    unnamed x27, local copies, waits for them, and re-layouts  9.91 us

profile of v1, /device:TPU:0, one launch (start us, length us, event | category | flops | bytes accessed | tf_op | source)
XLA Modules:
  0.0 47.7 jit_solution(11766205071276891389)
XLA Ops:
  0.6 0.0 copy-start.8
  0.6 0.0 copy-start.9
  0.7 0.0 copy-start.10
  0.7 0.0 copy-start.11
  0.7 0.6 %copy-done.8 = f32[5,12]{1,0:T(8,128)S(1)} copy-done((f32[5,12]{1,0:T(8,128)S(1)}, f32[5,12]{1,0:T(8,128)}, u32[]{:S(2)}) %copy-start.8) | copy-done | bytes 264
  1.3 0.0 copy-done.9
  1.3 0.0 copy-done.10
  1.3 0.0 copy-done.11
  1.3 0.0 copy-start
  1.3 1.1 %copy-done = bf16[12,16,16,128]{3,2,1,0:T(8,128)(2,1)S(1)} copy-done((bf16[12,16,16,128]{3,2,1,0:T(8,128)(2,1)S(1)}, bf16[12,16,16,128]{3,2,1,0:T(8,128)(2,1)}, u32[]{:S(2)}) %copy-start) | copy-done | bytes 786456
  2.5 0.0 copy-start.1
  2.5 0.9 %copy-done.1 = f32[16,32,128]{2,1,0:T(8,128)S(1)} copy-done((f32[16,32,128]{2,1,0:T(8,128)S(1)}, f32[16,32,128]{2,1,0:T(8,128)}, u32[]{:S(2)}) %copy-start.1) | copy-done | bytes 262168
  3.4 0.0 copy-start.2
  3.4 0.9 %copy-done.2 = f32[16,32,128]{2,1,0:T(8,128)S(1)} copy-done((f32[16,32,128]{2,1,0:T(8,128)S(1)}, f32[16,32,128]{2,1,0:T(8,128)}, u32[]{:S(2)}) %copy-start.2) | copy-done | bytes 262168
  4.4 0.0 copy-start.3
  4.4 0.9 %copy-done.3 = s32[16,32,128]{2,1,0:T(8,128)S(1)} copy-done((s32[16,32,128]{2,1,0:T(8,128)S(1)}, s32[16,32,128]{2,1,0:T(8,128)}, u32[]{:S(2)}) %copy-start.3) | copy-done | bytes 262168
  5.3 0.9 %copy-done.4 = f32[16,16,128]{2,1,0:T(8,128)S(1)} copy-done((f32[16,16,128]{2,1,0:T(8,128)S(1)}, f32[16,16,128]{2,1,0:T(8,128)}, u32[]{:S(2)}) %copy-start.4) | copy-done | bytes 131096
  6.2 0.9 %copy-done.5 = f32[16,16,128]{2,1,0:T(8,128)S(1)} copy-done((f32[16,16,128]{2,1,0:T(8,128)S(1)}, f32[16,16,128]{2,1,0:T(8,128)}, u32[]{:S(2)}) %copy-start.5) | copy-done | bytes 131096
  7.1 0.7 %copy-done.6 = s32[1,1,1,8,512]{4,3,2,1,0:T(8,128)S(1)} copy-done((s32[1,1,1,8,512]{4,3,2,1,0:T(8,128)S(1)}, s32[1,1,1,8,512]{4,3,2,1,0:T(8,128)}, u32[]{:S(2)}) %copy-start.6) | copy-done | bytes 16408
  7.9 0.7 %copy-done.7 = s32[1,1,1,8,512]{4,3,2,1,0:T(8,128)S(1)} copy-done((s32[1,1,1,8,512]{4,3,2,1,0:T(8,128)S(1)}, s32[1,1,1,8,512]{4,3,2,1,0:T(8,128)}, u32[]{:S(2)}) %copy-start.7) | copy-done | bytes 16408
  8.6 37.1 %shard_map.139 = (f32[16,16,128]{2,1,0:T(8,128)S(1)}, f32[16,16,128]{2,1,0:T(8,128)S(1)}, f32[16,32,128]{2,1,0:T(8,128)S(1)}) custom-call(bf16[12,16,16,128]{3,2,1,0:T(8,128)(2,1)S(1)} %copy-done, f32[16,16,128]{2,1,0:T(8,128)S(1)} %copy-done.4, f32[16,16,128]{2,1,0:T(8,128)S(1)} %copy-done.5, f32[5,12]{1,0:T(8,128)S(1)} %copy-done.8, ...), custom_call_target="tpu_custom_call" | custom-call | tf_op jit(solution)/shard_map/pallas_call | solution.py:487
  45.6 0.7 %copy.18 = f32[16,16,128]{2,1,0:T(8,128)} copy(f32[16,16,128]{2,1,0:T(8,128)S(1)} %get-tuple-element.6) | data formatting | bytes 262144
  46.3 0.7 %copy.19 = f32[16,16,128]{2,1,0:T(8,128)} copy(f32[16,16,128]{2,1,0:T(8,128)S(1)} %get-tuple-element.7) | data formatting | bytes 262144
  46.9 0.7 %copy.20 = f32[16,32,128]{2,1,0:T(8,128)} copy(f32[16,32,128]{2,1,0:T(8,128)S(1)} %get-tuple-element.8) | data formatting | bytes 524288
  (4 shorter events, 0.0 us)
Async XLA Ops:
  0.6 0.7 %copy-start.8 = (f32[5,12]{1,0:T(8,128)S(1)}, f32[5,12]{1,0:T(8,128)}, u32[]{:S(2)}) copy-start(f32[5,12]{1,0:T(8,128)} %ion_params.1) | copy-start | bytes 724
  0.6 0.7 %copy-start.9 = (f32[4]{0:T(128)S(1)}, f32[4]{0:T(128)}, u32[]{:S(2)}) copy-start(f32[4]{0:T(128)} %cond_table.1) | copy-start | bytes 52
  0.7 0.7 %copy-start.10 = (s32[1,1,1,8]{3,2,1,0:T(1,128)S(1)}, s32[1,1,1,8]{3,2,1,0:T(1,128)}, u32[]{:S(2)}) copy-start(s32[1,1,1,8]{3,2,1,0:T(1,128)} %param.21) | copy-start | bytes 100
  0.7 0.7 %copy-start.11 = (s32[1,1,1,8]{3,2,1,0:T(1,128)S(1)}, s32[1,1,1,8]{3,2,1,0:T(1,128)}, u32[]{:S(2)}) copy-start(s32[1,1,1,8]{3,2,1,0:T(1,128)} %param.23) | copy-start | bytes 100
  1.3 1.1 %copy-start = (bf16[12,16,16,128]{3,2,1,0:T(8,128)(2,1)S(1)}, bf16[12,16,16,128]{3,2,1,0:T(8,128)(2,1)}, u32[]{:S(2)}) copy-start(bf16[12,16,16,128]{3,2,1,0:T(8,128)(2,1)} %states.1) | copy-start | bytes 2359300
  2.5 0.9 %copy-start.1 = (f32[16,32,128]{2,1,0:T(8,128)S(1)}, f32[16,32,128]{2,1,0:T(8,128)}, u32[]{:S(2)}) copy-start(f32[16,32,128]{2,1,0:T(8,128)} %torso_phi.1) | copy-start | bytes 786436
  3.4 0.9 %copy-start.2 = (f32[16,32,128]{2,1,0:T(8,128)S(1)}, f32[16,32,128]{2,1,0:T(8,128)}, u32[]{:S(2)}) copy-start(f32[16,32,128]{2,1,0:T(8,128)} %tissue_scale.1) | copy-start | bytes 786436
  4.4 0.9 %copy-start.3 = (s32[16,32,128]{2,1,0:T(8,128)S(1)}, s32[16,32,128]{2,1,0:T(8,128)}, u32[]{:S(2)}) copy-start(s32[16,32,128]{2,1,0:T(8,128)} %labels.1) | copy-start | bytes 786436
  5.3 0.9 %copy-start.4 = (f32[16,16,128]{2,1,0:T(8,128)S(1)}, f32[16,16,128]{2,1,0:T(8,128)}, u32[]{:S(2)}) copy-start(f32[16,16,128]{2,1,0:T(8,128)} %membrane.1) | copy-start | bytes 393220
  6.2 0.9 %copy-start.5 = (f32[16,16,128]{2,1,0:T(8,128)S(1)}, f32[16,16,128]{2,1,0:T(8,128)}, u32[]{:S(2)}) copy-start(f32[16,16,128]{2,1,0:T(8,128)} %phi_heart.1) | copy-start | bytes 393220
  7.1 0.7 %copy-start.6 = (s32[1,1,1,8,512]{4,3,2,1,0:T(8,128)S(1)}, s32[1,1,1,8,512]{4,3,2,1,0:T(8,128)}, u32[]{:S(2)}) copy-start(s32[1,1,1,8,512]{4,3,2,1,0:T(8,128)} %param.20) | copy-start | bytes 49156
  7.9 0.7 %copy-start.7 = (s32[1,1,1,8,512]{4,3,2,1,0:T(8,128)S(1)}, s32[1,1,1,8,512]{4,3,2,1,0:T(8,128)}, u32[]{:S(2)}) copy-start(s32[1,1,1,8,512]{4,3,2,1,0:T(8,128)} %param.22) | copy-start | bytes 49156

commit v2 on v1

v2 whole, which is shorter than its diff:
```python
import functools

import jax
import jax.numpy as jnp
from jax import lax
from jax.experimental import pallas as pl
from jax.experimental.pallas import tpu as pltpu
from jax.sharding import PartitionSpec as P

LABELS = 4
SWEEPS_H = 3
SWEEPS_T = 4

time_step = 0.1
intra_cond = 0.25
extra_cond = 0.5
penalty = 2.0
cheb_low = 0.1
cheb_high = 2.0

MESH = pl.DeviceIdType.MESH
F32 = jnp.float32
BF16 = jnp.bfloat16


def cheb_coeffs(sweeps):
    centre = 0.5 * (cheb_high + cheb_low)
    half_width = 0.5 * (cheb_high - cheb_low)
    scaled = centre / half_width
    coeffs = [(0.0, 1.0 / centre)]
    rho_old = 1.0 / scaled
    for number in range(1, sweeps):
        rho_new = 1.0 / (2.0 * scaled - rho_old)
        coeffs.append((rho_new * rho_old, 2.0 * rho_new / half_width))
        rho_old = rho_new
    return coeffs


def harmonic(a, b):
    return 2.0 * a * b / (a + b)


def two_terms(values):
    high = values.astype(BF16)
    return high, (values - high.astype(F32)).astype(BF16)


class Grid:
    def __init__(self, shape, stage, landing, sends, recvs, ypad, place):
        self.shape = shape
        self.stage = stage
        self.landing = landing
        self.sends = sends
        self.recvs = recvs
        self.ypad = ypad
        self.place = place

    def clear_ends(self):
        for axis, (_, low, high) in enumerate(self.place):
            for side, (_, present) in enumerate((low, high)):
                if present is None:
                    continue

                @pl.when(jnp.logical_not(present))
                def _(axis=axis, side=side):
                    ref = self.landing[axis]
                    ref[side] = jnp.zeros(ref.shape[1:], F32)

    def pack(self, slot, field):
        nx, ny, nz = self.shape
        xs, ys, zs = self.stage
        xs[0, slot] = field[0]
        xs[1, slot] = field[nx - 1]
        ys[0, slot] = field[:, 0:1, :]
        ys[1, slot] = field[:, ny - 1 : ny, :]
        turned = jnp.transpose(field.reshape(nx * ny, nz))
        zs[0, slot] = turned[0:1, :]
        zs[1, slot] = turned[nz - 1 : nz, :]

    def copies(self, turn, first, count):
        for axis, (name, low, high) in enumerate(self.place):
            for side, there in enumerate((low, high)):
                back = (high, low)[side]
                yield (
                    pltpu.make_async_remote_copy(
                        src_ref=self.stage[axis].at[side, pl.ds(first, count)],
                        dst_ref=self.landing[axis].at[1 - side, pl.ds(first, count)],
                        send_sem=self.sends.at[turn, axis, side],
                        recv_sem=self.recvs.at[turn, axis, 1 - side],
                        device_id={name: there[0]},
                        device_id_type=MESH,
                    ),
                    there[1],
                    back[1],
                )

    def send(self, turn, first, count):
        for copy, out, _ in self.copies(turn, first, count):
            if out is None:
                copy.start()
            else:
                pl.when(out)(copy.start)

    def wait(self, turn, first, count):
        for copy, _, back in self.copies(turn, first, count):
            if back is None:
                copy.wait_recv()
            else:
                pl.when(back)(copy.wait_recv)

    def finish(self, turn, first, count):
        for copy, out, _ in self.copies(turn, first, count):
            if out is None:
                copy.wait_send()
            else:
                pl.when(out)(copy.wait_send)

    def around(self, slot, field):
        nx, ny, nz = self.shape
        rx, ry, rz = self.landing
        below_x = jnp.concatenate([rx[0, slot][None], field[:-1]], axis=0)
        above_x = jnp.concatenate([field[1:], rx[1, slot][None]], axis=0)
        self.ypad[:, 8 : 8 + ny, :] = field
        self.ypad[:, 7:8, :] = ry[0, slot]
        self.ypad[:, 8 + ny : 9 + ny, :] = ry[1, slot]
        below_y = self.ypad[:, 7 : 7 + ny, :]
        above_y = self.ypad[:, 9 : 9 + ny, :]
        depth = lax.broadcasted_iota(jnp.int32, (nz, nx * ny), 0)
        ends = jnp.transpose(jnp.where(depth == 0, rz[0, slot], rz[1, slot]))
        flat = field.reshape(nx * ny, nz)
        lanes = lax.broadcasted_iota(jnp.int32, (nx * ny, nz), 1)
        below_z = jnp.where(lanes == 0, ends, pltpu.roll(flat, 1, 1)).reshape(nx, ny, nz)
        above_z = jnp.where(lanes == nz - 1, ends, pltpu.roll(flat, nz - 1, 1)).reshape(nx, ny, nz)
        return below_x, above_x, below_y, above_y, below_z, above_z


def turned_table(layer, rows, width):
    high, low = two_terms(jnp.transpose(layer.reshape(rows, width)))
    return jnp.concatenate([high, low], axis=1)


class Patch:
    def __init__(self, nodes, counts, row_hots, columns, rows, width):
        self.nodes = nodes
        self.counts = counts
        self.row_hots = row_hots
        self.columns = columns
        self.rows = rows
        self.width = width
        self.cap = nodes.shape[1]

    def prepare(self, peer):
        index = self.nodes[pl.ds(peer, 1), :]
        slot_ids = lax.broadcasted_iota(jnp.int32, (1, self.cap), 1)
        index = jnp.where(slot_ids < self.counts[peer], index, -1)
        row_ids = lax.broadcasted_iota(jnp.int32, (self.rows, self.cap), 0)
        row = lax.shift_right_arithmetic(index, self.width.bit_length() - 1)
        self.row_hots[peer] = jnp.where(row_ids == row, 1.0, 0.0).astype(BF16)
        self.columns[peer] = index & (self.width - 1)

    def column_mask(self, peer):
        col_ids = lax.broadcasted_iota(jnp.int32, (self.width, self.cap), 0)
        return col_ids == self.columns[peer]

    def pick(self, table, peer):
        row_hot = self.row_hots[peer]
        chosen = jnp.dot(
            table, jnp.concatenate([row_hot, row_hot], axis=0), preferred_element_type=F32
        )
        return jnp.sum(jnp.where(self.column_mask(peer), chosen, 0.0), axis=0, keepdims=True)

    def weigh(self, peer):
        ones = jnp.where(self.column_mask(peer), 1.0, 0.0).astype(BF16)
        return lax.dot_general(
            self.row_hots[peer], ones, (((1,), (1,)), ((), ())), preferred_element_type=F32
        )

    def place_at(self, values, peer):
        mask = self.column_mask(peer)
        high = values.astype(BF16).astype(F32)
        low = values - high
        spread = jnp.concatenate(
            [jnp.where(mask, high, 0.0).astype(BF16), jnp.where(mask, low, 0.0).astype(BF16)],
            axis=0,
        )
        return lax.dot_general(
            self.row_hots[peer], spread, (((1,), (1,)), ((), ())), preferred_element_type=F32
        )


def kernel(
    sizes,
    states_in,
    membrane_in,
    phi_heart_in,
    ion_params_in,
    torso_phi_in,
    tissue_scale_in,
    labels_in,
    cond_table_in,
    send_node_in,
    send_count_in,
    recv_voxel_in,
    recv_count_in,
    new_membrane_out,
    heart_phi_out,
    torso_out_out,
    new_membrane, heart_phi, torso_out, store_sem,
    states, membrane, phi_heart, ion_params, torso_phi, tissue_scale, labels, cond_table,
    send_node, send_count, recv_voxel, recv_count, load_sem,
    hsx, hsy, hsz, hrx, hry, hrz, hypad, hsend, hrecv,
    tsx, tsy, tsz, trx, try_, trz, typad, tsend, trecv,
    sent, arrived, returned, came,
    out_sem, in_sem, back_sem, home_sem,
    phi_h, source_h, current_h, gains, update_t, right_t, weight_t,
    rows_node, cols_node, rows_voxel, cols_voxel,
):
    n_grp, n_gx, n_gy = sizes
    peers = n_gx * n_gy
    group = 8 if peers % 8 == 0 else 1
    g = lax.axis_index("grp")
    i = lax.axis_index("gx")
    j = lax.axis_index("gy")
    me = i * n_gy + j
    hshape = membrane.shape
    tshape = torso_phi.shape

    sources = (
        (membrane_in, membrane), (phi_heart_in, phi_heart), (tissue_scale_in, tissue_scale),
        (labels_in, labels), (cond_table_in, cond_table), (torso_phi_in, torso_phi),
        (ion_params_in, ion_params), (states_in, states), (send_node_in, send_node),
        (send_count_in, send_count), (recv_voxel_in, recv_voxel), (recv_count_in, recv_count),
    )
    stores = [
        pltpu.make_async_copy(new_membrane, new_membrane_out, store_sem.at[0]),
        pltpu.make_async_copy(torso_out, torso_out_out, store_sem.at[1]),
        pltpu.make_async_copy(heart_phi, heart_phi_out, store_sem.at[2]),
    ]
    loads = [
        pltpu.make_async_copy(there, here, load_sem.at[number])
        for number, (there, here) in enumerate(sources)
    ]
    for load in loads:
        load.start()

    place = (
        ("gx", (lax.rem(i + n_gx - 1, n_gx), None), (lax.rem(i + 1, n_gx), None)),
        ("gy", (jnp.maximum(j - 1, 0), j > 0), (jnp.minimum(j + 1, n_gy - 1), j < n_gy - 1)),
        ("grp", (jnp.maximum(g - 1, 0), g > 0), (jnp.minimum(g + 1, n_grp - 1), g < n_grp - 1)),
    )
    heart = Grid(hshape, (hsx, hsy, hsz), (hrx, hry, hrz), hsend, hrecv, hypad, place)
    torso = Grid(tshape, (tsx, tsy, tsz), (trx, try_, trz), tsend, trecv, typad, place)
    heart.clear_ends()
    torso.clear_ends()

    def peer_at(step):
        other = lax.rem(me + step, peers)
        return other, {"gx": other // n_gy, "gy": lax.rem(other, n_gy)}

    barrier = pltpu.get_barrier_semaphore()

    def greet(step, carry):
        pl.semaphore_signal(barrier, inc=1, device_id=peer_at(step)[1], device_id_type=MESH)
        return carry

    lax.fori_loop(1, peers, greet, 0, unroll=peers <= 8)
    _, low_z, high_z = place[2]
    for there, present in (low_z, high_z):

        @pl.when(present)
        def _(there=there):
            pl.semaphore_signal(barrier, inc=1, device_id={"grp": there}, device_id_type=MESH)

    loads[0].wait()
    voltage = membrane[...]
    heart.pack(0, voltage)
    loads[1].wait()
    heart.pack(1, phi_heart[...])
    pl.semaphore_wait(
        barrier, peers - 1 + (g > 0).astype(jnp.int32) + (g < n_grp - 1).astype(jnp.int32)
    )
    heart.send(0, 0, 2)

    for load in loads[2:6]:
        load.wait()
    names = labels[...]
    table = jnp.where(names == 0, cond_table[0], 0.0)
    for number in range(1, LABELS):
        table = jnp.where(names == number, cond_table[number], table)
    conduct = tissue_scale[...] * table
    torso.pack(0, conduct)
    torso.pack(1, torso_phi[...])
    torso.send(0, 0, 2)

    loads[6].wait()
    loads[7].wait()
    current = jnp.zeros(hshape, F32)
    for state in range(states.shape[0]):
        line = jnp.zeros((1, 1, hshape[2]), F32)
        half_slope = 0.5 / (line + ion_params[1, state])
        decay = jnp.exp(line - time_step * ion_params[2, state])
        steady = 0.5 + 0.5 * jnp.tanh((voltage - ion_params[0, state]) * half_slope)
        gate = steady + (states[state].astype(F32) - steady) * decay
        current = current + ion_params[3, state] * gate * (voltage - ion_params[4, state])
    current_h[...] = current

    ny = lax.broadcasted_iota(jnp.int32, hshape, 1) + j * hshape[1]
    nz = lax.broadcasted_iota(jnp.int32, hshape, 2) + g * hshape[2]
    diag = (
        6.0
        - jnp.where(ny == 0, 1.0, 0.0)
        - jnp.where(ny == hshape[1] * n_gy - 1, 1.0, 0.0)
        - jnp.where(nz == 0, 1.0, 0.0)
        - jnp.where(nz == hshape[2] * n_grp - 1, 1.0, 0.0)
    )
    inverse = 1.0 / diag

    def total_of(parts):
        return ((parts[0] + parts[1]) + (parts[2] + parts[3])) + (parts[4] + parts[5])

    layer_h = hshape[0] // 4
    rows_h = layer_h * hshape[1]
    layer = tshape[0] // 4
    rows = layer * tshape[1]
    width = tshape[2]
    nodes = Patch(send_node, send_count, rows_node, cols_node, rows_h, hshape[2])
    voxels = Patch(recv_voxel, recv_count, rows_voxel, cols_voxel, rows, width)

    def over_peers(body, start):
        def one_group(number, carry):
            for offset in range(group):
                carry = body(number * group + offset, carry)
            return carry

        if peers == group:
            return one_group(0, start)
        return lax.fori_loop(0, peers // group, one_group, start)

    def indices():
        for load in loads[8:]:
            load.wait()

        def prepare(peer, carry):
            nodes.prepare(peer)
            voxels.prepare(peer)
            return carry + voxels.weigh(peer)

        weight_t[...] = penalty * over_peers(prepare, jnp.zeros((rows, width), F32))

    def conductances():
        torso.wait(0, 0, 2)
        faces = [harmonic(conduct, other) for other in torso.around(0, conduct)]
        weight = weight_t[...].reshape(layer, tshape[1], width)
        total = total_of(faces)
        total = jnp.concatenate([total[:layer] + weight, total[layer:]], axis=0)
        scale = 1.0 / total
        for number in range(6):
            gains[number] = faces[number] * scale
        right_t[...] = penalty * scale[:layer]

    def torso_residue(slot, field):
        return -field + total_of(
            [gains[n] * other for n, other in enumerate(torso.around(slot, field))]
        )

    heart.wait(0, 0, 2)
    lap_mem = diag * voltage - total_of(heart.around(0, voltage))
    source_h[...] = lap_mem
    base = (-intra_cond / (intra_cond + extra_cond)) * lap_mem * inverse
    iterate = phi_heart[...]
    update = None
    for number, (carry_coef, resid_coef) in enumerate(cheb_coeffs(SWEEPS_H)):
        if number > 0:
            heart.wait(number, number + 1, 1)
        around = total_of(heart.around(number + 1, iterate))
        residue = base - iterate + around * inverse
        update = resid_coef * residue if update is None else carry_coef * update + resid_coef * residue
        iterate = iterate + update
        if number < SWEEPS_H - 1:
            heart.pack(number + 2, iterate)
            heart.send(number + 1, number + 2, 1)
        if number == 0:
            indices()
        if number == 1:
            conductances()
    phi_new = iterate
    phi_h[...] = phi_new

    def patch(other, source, target, sends, recvs, mine):
        return pltpu.make_async_remote_copy(
            src_ref=source.at[other],
            dst_ref=target.at[mine],
            send_sem=sends.at[other],
            recv_sem=recvs.at[mine],
            device_id={"gx": other // n_gy, "gy": lax.rem(other, n_gy)},
            device_id_type=MESH,
        )

    to_torso = (sent, arrived, out_sem, in_sem)
    to_heart = (returned, came, back_sem, home_sem)

    def post(buffers, fill):
        source, target = buffers[:2]

        def one_group(number, carry):
            picked = [fill(number * group + offset) for offset in range(group)]
            for offset in range(group):
                source[number * group + offset] = picked[offset]
            return carry

        if peers == group:
            one_group(0, 0)
        else:
            lax.fori_loop(0, peers // group, one_group, 0)

        def start(step, carry):
            patch(peer_at(step)[0], *buffers, me).start()
            return carry

        lax.fori_loop(1, peers, start, 0, unroll=peers <= 8)
        target[me] = source[me]

    def receive(buffers):
        def land(step, carry):
            other = peer_at(step)[0]
            patch(other, *buffers, other).wait_recv()
            return carry

        lax.fori_loop(1, peers, land, 0, unroll=peers <= 8)

    table_h = turned_table(phi_new[:layer_h], rows_h, hshape[2])
    post(to_torso, lambda peer: nodes.pick(table_h, peer))
    heart.pack(SWEEPS_H + 1, phi_new)
    heart.send(SWEEPS_H, SWEEPS_H + 1, 1)

    iterate = torso_phi[...]
    update_t[...] = torso_residue(1, iterate)

    receive(to_torso)
    summed = over_peers(
        lambda peer, carry: carry + voxels.place_at(arrived[peer], peer),
        jnp.zeros((rows, 2 * width), F32),
    )
    summed = summed[:, :width] + summed[:, width:]
    right = summed.reshape(layer, tshape[1], width) * right_t[...]
    right_t[...] = right

    coeffs = cheb_coeffs(SWEEPS_T)
    update = update_t[...]
    update = coeffs[0][1] * jnp.concatenate([update[:layer] + right, update[layer:]], axis=0)
    iterate = iterate + update
    for number in range(1, SWEEPS_T):
        torso.pack(number + 1, iterate)
        torso.send(number, number + 1, 1)
        if number == 1:
            phi_new = phi_h[...]
            heart.wait(SWEEPS_H, SWEEPS_H + 1, 1)
            lap_phi = diag * phi_new - total_of(heart.around(SWEEPS_H + 1, phi_new))
            new_membrane[...] = membrane[...] + time_step * (
                -intra_cond * (source_h[...] + lap_phi) - current_h[...]
            )
            stores[0].start()
        torso.wait(number, number + 1, 1)
        residue = torso_residue(number + 1, iterate)
        residue = jnp.concatenate([residue[:layer] + right_t[...], residue[layer:]], axis=0)
        update = coeffs[number][0] * update + coeffs[number][1] * residue
        iterate = iterate + update
    table_t = turned_table(iterate[:layer], rows, width)
    post(
        to_heart, lambda peer: penalty * (arrived[peer] - voxels.pick(table_t, peer))
    )
    torso_out[...] = iterate
    stores[1].start()
    phi_new = phi_h[...]
    heart_phi[...] = phi_new

    heart.finish(0, 0, 2)
    torso.finish(0, 0, 2)
    for number in range(1, SWEEPS_H + 1):
        heart.finish(number, number + 1, 1)
    for number in range(1, SWEEPS_T):
        torso.finish(number, number + 1, 1)

    receive(to_heart)
    flux = over_peers(
        lambda peer, carry: carry + nodes.place_at(came[peer], peer),
        jnp.zeros((rows_h, 2 * hshape[2]), F32),
    )
    flux = (flux[:, : hshape[2]] + flux[:, hshape[2] :]).reshape(layer_h, hshape[1], hshape[2])
    heart_phi[0:layer_h] = phi_new[:layer_h] - flux * (
        inverse[:layer_h] * (1.0 / (intra_cond + extra_cond))
    )
    stores[2].start()

    def settle(step, carry):
        other = peer_at(step)[0]
        patch(other, *to_torso, other).wait_send()
        patch(other, *to_heart, other).wait_send()
        return carry

    lax.fori_loop(1, peers, settle, 0, unroll=peers <= 8)
    for store in stores:
        store.wait()


def write_out(first, second, third, first_out, second_out, third_out, sems):
    copies = [
        pltpu.make_async_copy(here, there, sems.at[number])
        for number, (here, there) in enumerate(
            ((first, first_out), (second, second_out), (third, third_out))
        )
    ]
    for copy in copies:
        copy.start()
    for copy in copies:
        copy.wait()


def per_device(sizes, *args):
    peers, cap = args[8].shape[-2:]
    args = list(args)
    for number in (8, 10):
        args[number] = args[number].reshape(peers, cap)
    for number in (9, 11):
        args[number] = args[number].reshape(peers)
    hshape = args[1].shape
    tshape = args[4].shape
    hx, hy, hz = hshape
    tx, ty, tz = tshape
    hbm = pl.BlockSpec(memory_space=pltpu.HBM)
    in_smem = (3, 7, 9, 11)

    def grid_scratch(shape, slots, turns):
        nx, ny, nz = shape
        faces = [
            pltpu.VMEM((2, slots, ny, nz), F32),
            pltpu.VMEM((2, slots, nx, 1, nz), F32),
            pltpu.VMEM((2, slots, 1, nx * ny), F32),
        ]
        return (
            faces
            + faces
            + [
                pltpu.VMEM((nx, ny + 16, nz), F32),
                pltpu.SemaphoreType.DMA((turns, 3, 2)),
                pltpu.SemaphoreType.DMA((turns, 3, 2)),
            ]
        )

    staged = [
        pltpu.VMEM(hshape, F32),
        pltpu.VMEM(hshape, F32),
        pltpu.VMEM(tshape, F32),
        pltpu.SemaphoreType.DMA((3,)),
    ] + [
        (pltpu.SMEM if number in in_smem else pltpu.VMEM)(array.shape, array.dtype)
        for number, array in enumerate(args)
    ] + [pltpu.SemaphoreType.DMA((len(args),))]
    patches = [pltpu.VMEM((peers, 1, cap), F32)] * 4
    signals = [pltpu.SemaphoreType.DMA((peers,))] * 4
    rows_h = hx // 4 * hy
    rows = tx // 4 * ty
    work = [
        pltpu.VMEM(hshape, F32),
        pltpu.VMEM(hshape, F32),
        pltpu.VMEM(hshape, F32),
        pltpu.VMEM((6, tx, ty, tz), F32),
        pltpu.VMEM(tshape, F32),
        pltpu.VMEM((tx // 4, ty, tz), F32),
        pltpu.VMEM((rows, tz), F32),
        pltpu.VMEM((peers, rows_h, cap), BF16),
        pltpu.VMEM((peers, 1, cap), jnp.int32),
        pltpu.VMEM((peers, rows, cap), BF16),
        pltpu.VMEM((peers, 1, cap), jnp.int32),
    ]
    shapes = tuple(jax.ShapeDtypeStruct(shape, F32) for shape in (hshape, hshape, tshape))
    results = pl.pallas_call(
        functools.partial(kernel, sizes),
        out_shape=shapes,
        in_specs=[hbm] * len(args),
        out_specs=(hbm, hbm, hbm),
        scratch_shapes=staged
        + grid_scratch(hshape, SWEEPS_H + 2, SWEEPS_H + 1)
        + grid_scratch(tshape, SWEEPS_T + 1, SWEEPS_T)
        + patches
        + signals
        + work,
        compiler_params=pltpu.CompilerParams(
            collective_id=0, has_side_effects=True, vmem_limit_bytes=64 * 1024 * 1024
        ),
    )(*args)
    return pl.pallas_call(
        write_out,
        out_shape=shapes,
        in_specs=[hbm, hbm, hbm],
        out_specs=(hbm, hbm, hbm),
        scratch_shapes=[pltpu.SemaphoreType.DMA((3,))],
        compiler_params=pltpu.CompilerParams(vmem_limit_bytes=64 * 1024 * 1024),
    )(*results)


def solution(mesh):
    sizes = (mesh.shape["grp"], mesh.shape["gx"], mesh.shape["gy"])
    placed = (
        P(None, "gx", "gy", "grp"),
        P("gx", "gy", "grp"),
        P("gx", "gy", "grp"),
        P(),
        P("gx", "gy", "grp"),
        P("gx", "gy", "grp"),
        P("gx", "gy", "grp"),
        P(),
        P("grp", "gx", "gy", None, None),
        P("grp", "gx", "gy", None),
        P("grp", "gx", "gy", None, None),
        P("grp", "gx", "gy", None),
    )
    return jax.shard_map(
        functools.partial(per_device, sizes),
        mesh=mesh,
        in_specs=placed,
        out_specs=(P("gx", "gy", "grp"), P("gx", "gy", "grp"), P("gx", "gy", "grp")),
        check_vma=False,
    )
```

time: 48.2 us -> 53.8 us (1.12)
  Pallas kernels: 37.1 us -> 53 us
  local copies, waits for them, and re-layouts: 9.91 us -> 0 us
    pallas_call x1 -> x2, Pallas kernels: 37.1 us -> 53 us  [the longest x1 36 us: per_device(): pl.pallas_call(functools.partial(kernel, sizes), out_shape=shapes, in_spe...]
    unnamed x27 -> x0, local copies, waits for them, and re-layouts: 9.91 us -> none
where the time goes in v2:
time: 53.8 us; the launch traced here: 53.6 us
  Pallas kernels  53 us (99%)
  between operations  0.64 us (1%)
    pallas_call x1, Pallas kernels, per_device(): pl.pallas_call(functools.partial(kernel, sizes), out_shape=shapes, in_spe...  36 us
    pallas_call x1, Pallas kernels, per_device(): pl.pallas_call(write_out, out_shape=shapes, in_specs=[hbm, hbm, hbm], out...  17 us

profile of v2, /device:TPU:0, one launch (start us, length us, event | category | flops | bytes accessed | tf_op | source)
XLA Modules:
  0.0 53.6 jit_solution(1104127388876591037)
XLA Ops:
  0.6 36.0 %shard_map.139 = (f32[16,16,128]{2,1,0:T(8,128)}, f32[16,16,128]{2,1,0:T(8,128)}, f32[16,32,128]{2,1,0:T(8,128)}) custom-call(bf16[12,16,16,128]{3,2,1,0:T(8,128)(2,1)} %states_in.1, f32[16,16,128]{2,1,0:T(8,128)} %membrane_in.1, f32[16,16,128]{2,1,0:T(8,128)} %phi_heart_in.1, f32[5,12]{1,0:T(8,128)} %ion_params_in.1, f32[16,32,128]{2,1,0:T(8,128)} %torso_phi_in.1, ...), custom_call_target="tpu_custom_call" | custom-call | tf_op jit(solution)/shard_map/pallas_call | solution.py:577
  36.6 17.0 %shard_map.140 = (f32[16,16,128]{2,1,0:T(8,128)}, f32[16,16,128]{2,1,0:T(8,128)}, f32[16,32,128]{2,1,0:T(8,128)}) custom-call(f32[16,16,128]{2,1,0:T(8,128)} %get-tuple-element.6.first, f32[16,16,128]{2,1,0:T(8,128)} %get-tuple-element.7.second, f32[16,32,128]{2,1,0:T(8,128)} %get-tuple-element.8.third), custom_call_target="tpu_custom_call" | custom-call | tf_op jit(solution)/shard_map/pallas_call | solution.py:592

commit v3 on v2

--- a/solution.py
+++ b/solution.py
@@ -46,16 +46,20 @@
 
 
 class Grid:
-    def __init__(self, shape, stage, landing, sends, recvs, ypad, place):
+    def __init__(self, shape, stage, landing, sends, recvs, ypad, place, partial):
         self.shape = shape
         self.stage = stage
         self.landing = landing
         self.sends = sends
         self.recvs = recvs
         self.ypad = ypad
+        self.partial = partial
         self.place = place
 
     def clear_ends(self):
+        nx, ny, nz = self.shape
+        self.ypad[:, 7:8, :] = jnp.zeros((nx, 1, nz), F32)
+        self.ypad[:, 8 + ny : 9 + ny, :] = jnp.zeros((nx, 1, nz), F32)
         for axis, (_, low, high) in enumerate(self.place):
             for side, (_, present) in enumerate((low, high)):
                 if present is None:
@@ -115,23 +119,69 @@
             else:
                 pl.when(out)(copy.wait_send)
 
+    def inside(self, field):
+        nx, ny, nz = self.shape
+        none = jnp.zeros((1, ny, nz), F32)
+        below_x = jnp.concatenate([none, field[:-1]], axis=0)
+        above_x = jnp.concatenate([field[1:], none], axis=0)
+        self.ypad[:, 8 : 8 + ny, :] = field
+        below_y = self.ypad[:, 7 : 7 + ny, :]
+        above_y = self.ypad[:, 9 : 9 + ny, :]
+        flat = field.reshape(nx * ny, nz)
+        lanes = lax.broadcasted_iota(jnp.int32, (nx * ny, nz), 1)
+        below_z = jnp.where(lanes == 0, 0.0, pltpu.roll(flat, 1, 1)).reshape(nx, ny, nz)
+        above_z = jnp.where(lanes == nz - 1, 0.0, pltpu.roll(flat, nz - 1, 1)).reshape(nx, ny, nz)
+        return below_x, above_x, below_y, above_y, below_z, above_z
+
+    def begin(self, field, gains=None, which=0):
+        parts = self.inside(field)
+        if gains is not None:
+            parts = [gains[number] * part for number, part in enumerate(parts)]
+        self.partial[which] = total_of(parts)
+
+    def ends(self, slot):
+        nx, ny, nz = self.shape
+        rz = self.landing[2]
+        depth = lax.broadcasted_iota(jnp.int32, (nz, nx * ny), 0)
+        turned = jnp.where(depth == 0, rz[0, slot], jnp.where(depth == nz - 1, rz[1, slot], 0.0))
+        return jnp.transpose(turned).reshape(nx, ny, nz)
+
+    def complete(self, slot, gains=None, end_gain=None, which=0):
+        nx, ny, nz = self.shape
+        rx, ry, _ = self.landing
+        ends = self.ends(slot)
+        for side, at in ((0, 0), (1, nx - 1)):
+            other = rx[side, slot]
+            if gains is not None:
+                other = gains[side, at] * other
+            self.partial[which, at] = self.partial[which, at] + other
+        for side, at in ((0, 0), (1, ny - 1)):
+            other = ry[side, slot]
+            if gains is not None:
+                other = gains[2 + side, :, at : at + 1, :] * other
+            self.partial[which, :, at : at + 1, :] = self.partial[which, :, at : at + 1, :] + other
+        if end_gain is not None:
+            ends = end_gain[...] * ends
+        return self.partial[which] + ends
+
     def around(self, slot, field):
         nx, ny, nz = self.shape
-        rx, ry, rz = self.landing
-        below_x = jnp.concatenate([rx[0, slot][None], field[:-1]], axis=0)
-        above_x = jnp.concatenate([field[1:], rx[1, slot][None]], axis=0)
-        self.ypad[:, 8 : 8 + ny, :] = field
-        self.ypad[:, 7:8, :] = ry[0, slot]
-        self.ypad[:, 8 + ny : 9 + ny, :] = ry[1, slot]
-        below_y = self.ypad[:, 7 : 7 + ny, :]
-        above_y = self.ypad[:, 9 : 9 + ny, :]
-        depth = lax.broadcasted_iota(jnp.int32, (nz, nx * ny), 0)
-        ends = jnp.transpose(jnp.where(depth == 0, rz[0, slot], rz[1, slot]))
-        flat = field.reshape(nx * ny, nz)
-        lanes = lax.broadcasted_iota(jnp.int32, (nx * ny, nz), 1)
-        below_z = jnp.where(lanes == 0, ends, pltpu.roll(flat, 1, 1)).reshape(nx, ny, nz)
-        above_z = jnp.where(lanes == nz - 1, ends, pltpu.roll(flat, nz - 1, 1)).reshape(nx, ny, nz)
+        rx, ry, _ = self.landing
+        below_x, above_x, below_y, above_y, below_z, above_z = self.inside(field)
+        below_x = jnp.concatenate([rx[0, slot][None], below_x[1:]], axis=0)
+        above_x = jnp.concatenate([above_x[:-1], rx[1, slot][None]], axis=0)
+        rows = lax.broadcasted_iota(jnp.int32, (nx, ny, nz), 1)
+        below_y = jnp.where(rows == 0, ry[0, slot], below_y)
+        above_y = jnp.where(rows == ny - 1, ry[1, slot], above_y)
+        lanes = lax.broadcasted_iota(jnp.int32, (nx, ny, nz), 2)
+        ends = self.ends(slot)
+        below_z = jnp.where(lanes == 0, ends, below_z)
+        above_z = jnp.where(lanes == nz - 1, ends, above_z)
         return below_x, above_x, below_y, above_y, below_z, above_z
+
+
+def total_of(parts):
+    return ((parts[0] + parts[1]) + (parts[2] + parts[3])) + (parts[4] + parts[5])
 
 
 def turned_table(layer, rows, width):
@@ -212,7 +262,7 @@
     tsx, tsy, tsz, trx, try_, trz, typad, tsend, trecv,
     sent, arrived, returned, came,
     out_sem, in_sem, back_sem, home_sem,
-    phi_h, source_h, current_h, gains, update_t, right_t, weight_t,
+    hpart, tpart, end_gain, phi_h, source_h, current_h, gains, right_t, weight_t,
     rows_node, cols_node, rows_voxel, cols_voxel,
 ):
     n_grp, n_gx, n_gy = sizes
@@ -231,10 +281,14 @@
         (ion_params_in, ion_params), (states_in, states), (send_node_in, send_node),
         (send_count_in, send_count), (recv_voxel_in, recv_voxel), (recv_count_in, recv_count),
     )
+    layer_h = hshape[0] // 4
+    surface = pl.ds(0, layer_h)
+    deep = pl.ds(layer_h, hshape[0] - layer_h)
     stores = [
         pltpu.make_async_copy(new_membrane, new_membrane_out, store_sem.at[0]),
         pltpu.make_async_copy(torso_out, torso_out_out, store_sem.at[1]),
-        pltpu.make_async_copy(heart_phi, heart_phi_out, store_sem.at[2]),
+        pltpu.make_async_copy(heart_phi.at[deep], heart_phi_out.at[deep], store_sem.at[2]),
+        pltpu.make_async_copy(heart_phi.at[surface], heart_phi_out.at[surface], store_sem.at[3]),
     ]
     loads = [
         pltpu.make_async_copy(there, here, load_sem.at[number])
@@ -248,8 +302,8 @@
         ("gy", (jnp.maximum(j - 1, 0), j > 0), (jnp.minimum(j + 1, n_gy - 1), j < n_gy - 1)),
         ("grp", (jnp.maximum(g - 1, 0), g > 0), (jnp.minimum(g + 1, n_grp - 1), g < n_grp - 1)),
     )
-    heart = Grid(hshape, (hsx, hsy, hsz), (hrx, hry, hrz), hsend, hrecv, hypad, place)
-    torso = Grid(tshape, (tsx, tsy, tsz), (trx, try_, trz), tsend, trecv, typad, place)
+    heart = Grid(hshape, (hsx, hsy, hsz), (hrx, hry, hrz), hsend, hrecv, hypad, place, hpart)
+    torso = Grid(tshape, (tsx, tsy, tsz), (trx, try_, trz), tsend, trecv, typad, place, tpart)
     heart.clear_ends()
     torso.clear_ends()
 
@@ -292,17 +346,20 @@
     torso.pack(1, torso_phi[...])
     torso.send(0, 0, 2)
 
-    loads[6].wait()
-    loads[7].wait()
-    current = jnp.zeros(hshape, F32)
-    for state in range(states.shape[0]):
-        line = jnp.zeros((1, 1, hshape[2]), F32)
-        half_slope = 0.5 / (line + ion_params[1, state])
-        decay = jnp.exp(line - time_step * ion_params[2, state])
-        steady = 0.5 + 0.5 * jnp.tanh((voltage - ion_params[0, state]) * half_slope)
-        gate = steady + (states[state].astype(F32) - steady) * decay
-        current = current + ion_params[3, state] * gate * (voltage - ion_params[4, state])
-    current_h[...] = current
+    def ionic(first, last):
+        voltage = membrane[...]
+        current = jnp.zeros(hshape, F32) if first == 0 else current_h[...]
+        for state in range(first, last):
+            line = jnp.zeros((1, 1, hshape[2]), F32)
+            half_slope = 0.5 / (line + ion_params[1, state])
+            decay = jnp.exp(line - time_step * ion_params[2, state])
+            steady = 0.5 + 0.5 * jnp.tanh((voltage - ion_params[0, state]) * half_slope)
+            gate = steady + (states[state].astype(F32) - steady) * decay
+            current = current + ion_params[3, state] * gate * (voltage - ion_params[4, state])
+        current_h[...] = current
+
+    heart.begin(voltage, which=0)
+    heart.begin(phi_heart[...], which=1)
 
     ny = lax.broadcasted_iota(jnp.int32, hshape, 1) + j * hshape[1]
     nz = lax.broadcasted_iota(jnp.int32, hshape, 2) + g * hshape[2]
@@ -315,10 +372,6 @@
     )
     inverse = 1.0 / diag
 
-    def total_of(parts):
-        return ((parts[0] + parts[1]) + (parts[2] + parts[3])) + (parts[4] + parts[5])
-
-    layer_h = hshape[0] // 4
     rows_h = layer_h * hshape[1]
     layer = tshape[0] // 4
     rows = layer * tshape[1]
@@ -356,15 +409,15 @@
         scale = 1.0 / total
         for number in range(6):
             gains[number] = faces[number] * scale
+        lanes = lax.broadcasted_iota(jnp.int32, tshape, 2)
+        end_gain[...] = jnp.where(
+            lanes == 0, faces[4] * scale, jnp.where(lanes == width - 1, faces[5] * scale, 0.0)
+        )
         right_t[...] = penalty * scale[:layer]
 
-    def torso_residue(slot, field):
-        return -field + total_of(
-            [gains[n] * other for n, other in enumerate(torso.around(slot, field))]
-        )
-
+    indices()
     heart.wait(0, 0, 2)
-    lap_mem = diag * voltage - total_of(heart.around(0, voltage))
+    lap_mem = diag * voltage - heart.complete(0, which=0)
     source_h[...] = lap_mem
     base = (-intra_cond / (intra_cond + extra_cond)) * lap_mem * inverse
     iterate = phi_heart[...]
@@ -372,17 +425,20 @@
     for number, (carry_coef, resid_coef) in enumerate(cheb_coeffs(SWEEPS_H)):
         if number > 0:
             heart.wait(number, number + 1, 1)
-        around = total_of(heart.around(number + 1, iterate))
+        around = heart.complete(number + 1, which=1)
         residue = base - iterate + around * inverse
         update = resid_coef * residue if update is None else carry_coef * update + resid_coef * residue
         iterate = iterate + update
         if number < SWEEPS_H - 1:
             heart.pack(number + 2, iterate)
             heart.send(number + 1, number + 2, 1)
+            heart.begin(iterate, which=1)
         if number == 0:
-            indices()
+            conductances()
         if number == 1:
-            conductances()
+            torso.begin(torso_phi[...], gains)
+            partial = torso.complete(1, gains, end_gain)
+            tpart[0] = partial
     phi_new = iterate
     phi_h[...] = phi_new
 
@@ -433,9 +489,11 @@
     heart.pack(SWEEPS_H + 1, phi_new)
     heart.send(SWEEPS_H, SWEEPS_H + 1, 1)
 
-    iterate = torso_phi[...]
-    update_t[...] = torso_residue(1, iterate)
-
+    heart.begin(phi_new, which=1)
+    half = states.shape[0] // 2
+    loads[6].wait()
+    loads[7].wait()
+    ionic(0, half)
     receive(to_torso)
     summed = over_peers(
         lambda peer, carry: carry + voxels.place_at(arrived[peer], peer),
@@ -446,22 +504,29 @@
     right_t[...] = right
 
     coeffs = cheb_coeffs(SWEEPS_T)
-    update = update_t[...]
+    iterate = torso_phi[...]
+    update = tpart[0] - iterate
     update = coeffs[0][1] * jnp.concatenate([update[:layer] + right, update[layer:]], axis=0)
     iterate = iterate + update
     for number in range(1, SWEEPS_T):
         torso.pack(number + 1, iterate)
         torso.send(number, number + 1, 1)
+        torso.begin(iterate, gains)
         if number == 1:
+            ionic(half, states.shape[0])
+        if number == 2:
             phi_new = phi_h[...]
             heart.wait(SWEEPS_H, SWEEPS_H + 1, 1)
-            lap_phi = diag * phi_new - total_of(heart.around(SWEEPS_H + 1, phi_new))
+            lap_phi = diag * phi_new - heart.complete(SWEEPS_H + 1, which=1)
             new_membrane[...] = membrane[...] + time_step * (
                 -intra_cond * (source_h[...] + lap_phi) - current_h[...]
             )
             stores[0].start()
+        if number == SWEEPS_T - 1:
+            heart_phi[layer_h:] = phi_h[layer_h:]
+            stores[2].start()
         torso.wait(number, number + 1, 1)
-        residue = torso_residue(number + 1, iterate)
+        residue = torso.complete(number + 1, gains, end_gain) - iterate
         residue = jnp.concatenate([residue[:layer] + right_t[...], residue[layer:]], axis=0)
         update = coeffs[number][0] * update + coeffs[number][1] * residue
         iterate = iterate + update
@@ -472,7 +537,6 @@
     torso_out[...] = iterate
     stores[1].start()
     phi_new = phi_h[...]
-    heart_phi[...] = phi_new
 
     heart.finish(0, 0, 2)
     torso.finish(0, 0, 2)
@@ -490,7 +554,7 @@
     heart_phi[0:layer_h] = phi_new[:layer_h] - flux * (
         inverse[:layer_h] * (1.0 / (intra_cond + extra_cond))
     )
-    stores[2].start()
+    stores[3].start()
 
     def settle(step, carry):
         other = peer_at(step)[0]
@@ -503,16 +567,22 @@
         store.wait()
 
 
-def write_out(first, second, third, first_out, second_out, third_out, sems):
-    copies = [
-        pltpu.make_async_copy(here, there, sems.at[number])
-        for number, (here, there) in enumerate(
-            ((first, first_out), (second, second_out), (third, third_out))
-        )
+def write_out(*refs):
+    sources, targets, held, (sems,) = refs[:3], refs[3:6], refs[6:9], refs[9:]
+    ins = [
+        pltpu.make_async_copy(there, here, sems.at[0, number])
+        for number, (there, here) in enumerate(zip(sources, held))
     ]
-    for copy in copies:
+    outs = [
+        pltpu.make_async_copy(here, there, sems.at[1, number])
+        for number, (here, there) in enumerate(zip(held, targets))
+    ]
+    for copy in ins:
         copy.start()
-    for copy in copies:
+    for copy, after in zip(ins, outs):
+        copy.wait()
+        after.start()
+    for copy in outs:
         copy.wait()
 
 
@@ -551,7 +621,7 @@
         pltpu.VMEM(hshape, F32),
         pltpu.VMEM(hshape, F32),
         pltpu.VMEM(tshape, F32),
-        pltpu.SemaphoreType.DMA((3,)),
+        pltpu.SemaphoreType.DMA((4,)),
     ] + [
         (pltpu.SMEM if number in in_smem else pltpu.VMEM)(array.shape, array.dtype)
         for number, array in enumerate(args)
@@ -561,11 +631,13 @@
     rows_h = hx // 4 * hy
     rows = tx // 4 * ty
     work = [
+        pltpu.VMEM((2,) + hshape, F32),
+        pltpu.VMEM((1,) + tshape, F32),
+        pltpu.VMEM(tshape, F32),
         pltpu.VMEM(hshape, F32),
         pltpu.VMEM(hshape, F32),
         pltpu.VMEM(hshape, F32),
         pltpu.VMEM((6, tx, ty, tz), F32),
-        pltpu.VMEM(tshape, F32),
         pltpu.VMEM((tx // 4, ty, tz), F32),
         pltpu.VMEM((rows, tz), F32),
         pltpu.VMEM((peers, rows_h, cap), BF16),
@@ -594,7 +666,8 @@
         out_shape=shapes,
         in_specs=[hbm, hbm, hbm],
         out_specs=(hbm, hbm, hbm),
-        scratch_shapes=[pltpu.SemaphoreType.DMA((3,))],
+        scratch_shapes=[pltpu.VMEM(array.shape, F32) for array in shapes]
+        + [pltpu.SemaphoreType.DMA((2, 3))],
         compiler_params=pltpu.CompilerParams(vmem_limit_bytes=64 * 1024 * 1024),
     )(*results)
 

time: 53.8 us -> 37.8 us (0.70)
  Pallas kernels: 53 us -> 37 us
    pallas_call x1, Pallas kernels: 17 us -> 1.84 us  [per_device(): pl.pallas_call(write_out, out_shape=shapes, in_specs=[hbm, hbm, hbm], out...]
    pallas_call x1, Pallas kernels: 36 us -> 35.2 us  [per_device(): pl.pallas_call(functools.partial(kernel, sizes), out_shape=shapes, in_spe...]
where the time goes in v3:
time: 37.8 us; the launch traced here: 37.7 us
  Pallas kernels  37 us (98%)
  between operations  0.64 us (2%)
    pallas_call x1, Pallas kernels, per_device(): pl.pallas_call(functools.partial(kernel, sizes), out_shape=shapes, in_spe...  35.2 us
    pallas_call x1, Pallas kernels, per_device(): pl.pallas_call(write_out, out_shape=shapes, in_specs=[hbm, hbm, hbm], out...  1.84 us

profile of v3, /device:TPU:0, one launch (start us, length us, event | category | flops | bytes accessed | tf_op | source)
XLA Modules:
  0.0 37.7 jit_solution(11992904930246519712)
XLA Ops:
  0.6 35.2 %shard_map.139 = (f32[16,16,128]{2,1,0:T(8,128)}, f32[16,16,128]{2,1,0:T(8,128)}, f32[16,32,128]{2,1,0:T(8,128)}) custom-call(bf16[12,16,16,128]{3,2,1,0:T(8,128)(2,1)} %states_in.1, f32[16,16,128]{2,1,0:T(8,128)} %membrane_in.1, f32[16,16,128]{2,1,0:T(8,128)} %phi_heart_in.1, f32[5,12]{1,0:T(8,128)} %ion_params_in.1, f32[16,32,128]{2,1,0:T(8,128)} %torso_phi_in.1, ...), custom_call_target="tpu_custom_call" | custom-call | tf_op jit(solution)/shard_map/pallas_call | solution.py:649
  35.8 1.8 %shard_map.140 = (f32[16,16,128]{2,1,0:T(8,128)}, f32[16,16,128]{2,1,0:T(8,128)}, f32[16,32,128]{2,1,0:T(8,128)}) custom-call(f32[16,16,128]{2,1,0:T(8,128)} %get-tuple-element.6.refs_0_, f32[16,16,128]{2,1,0:T(8,128)} %get-tuple-element.7.refs_1_, f32[16,32,128]{2,1,0:T(8,128)} %get-tuple-element.8.refs_2_), custom_call_target="tpu_custom_call" | custom-call | tf_op jit(solution)/shard_map/pallas_call | solution.py:664

commit v4 on v3

--- a/solution.py
+++ b/solution.py
@@ -46,7 +46,7 @@
 
 
 class Grid:
-    def __init__(self, shape, stage, landing, sends, recvs, ypad, place, partial):
+    def __init__(self, shape, stage, landing, sends, recvs, ypad, place, partial, ends, unroll):
         self.shape = shape
         self.stage = stage
         self.landing = landing
@@ -54,12 +54,12 @@
         self.recvs = recvs
         self.ypad = ypad
         self.partial = partial
+        self.ends = ends
+        self.unroll = unroll
         self.place = place
 
     def clear_ends(self):
-        nx, ny, nz = self.shape
-        self.ypad[:, 7:8, :] = jnp.zeros((nx, 1, nz), F32)
-        self.ypad[:, 8 + ny : 9 + ny, :] = jnp.zeros((nx, 1, nz), F32)
+        self.clear_faces()
         for axis, (_, low, high) in enumerate(self.place):
             for side, (_, present) in enumerate((low, high)):
                 if present is None:
@@ -119,37 +119,56 @@
             else:
                 pl.when(out)(copy.wait_send)
 
-    def inside(self, field):
-        nx, ny, nz = self.shape
-        none = jnp.zeros((1, ny, nz), F32)
-        below_x = jnp.concatenate([none, field[:-1]], axis=0)
-        above_x = jnp.concatenate([field[1:], none], axis=0)
-        self.ypad[:, 8 : 8 + ny, :] = field
-        below_y = self.ypad[:, 7 : 7 + ny, :]
-        above_y = self.ypad[:, 9 : 9 + ny, :]
-        flat = field.reshape(nx * ny, nz)
-        lanes = lax.broadcasted_iota(jnp.int32, (nx * ny, nz), 1)
-        below_z = jnp.where(lanes == 0, 0.0, pltpu.roll(flat, 1, 1)).reshape(nx, ny, nz)
-        above_z = jnp.where(lanes == nz - 1, 0.0, pltpu.roll(flat, nz - 1, 1)).reshape(nx, ny, nz)
-        return below_x, above_x, below_y, above_y, below_z, above_z
-
-    def begin(self, field, gains=None, which=0):
-        parts = self.inside(field)
-        if gains is not None:
-            parts = [gains[number] * part for number, part in enumerate(parts)]
-        self.partial[which] = total_of(parts)
-
-    def ends(self, slot):
+    def planes(self, body):
+        def one(at, carry):
+            body(at)
+            return carry
+
+        lax.fori_loop(0, self.shape[0], one, 0, unroll=self.unroll)
+
+    def get(self, at):
+        return self.ypad[at + 1, 8 : 8 + self.shape[1], :]
+
+    def put(self, at, plane):
+        self.ypad[at + 1, 8 : 8 + self.shape[1], :] = plane
+
+    def field(self):
+        nx, ny, _ = self.shape
+        return self.ypad[1 : nx + 1, 8 : 8 + ny, :]
+
+    def inside(self, at):
+        _, ny, nz = self.shape
+        lanes = lax.broadcasted_iota(jnp.int32, (ny, nz), 1)
+        plane = self.get(at)
+        return [
+            self.get(at - 1),
+            self.get(at + 1),
+            self.ypad[at + 1, 7 : 7 + ny, :],
+            self.ypad[at + 1, 9 : 9 + ny, :],
+            jnp.where(lanes == 0, 0.0, pltpu.roll(plane, 1, 1)),
+            jnp.where(lanes == nz - 1, 0.0, pltpu.roll(plane, nz - 1, 1)),
+        ]
+
+    def begin(self, gains=None, which=0):
+        def body(at):
+            parts = self.inside(at)
+            if gains is not None:
+                parts = [gains[number, at] * part for number, part in enumerate(parts)]
+            self.partial[which, at] = total_of(parts)
+
+        self.planes(body)
+
+    def turn_ends(self, slot):
         nx, ny, nz = self.shape
         rz = self.landing[2]
         depth = lax.broadcasted_iota(jnp.int32, (nz, nx * ny), 0)
         turned = jnp.where(depth == 0, rz[0, slot], jnp.where(depth == nz - 1, rz[1, slot], 0.0))
-        return jnp.transpose(turned).reshape(nx, ny, nz)
-
-    def complete(self, slot, gains=None, end_gain=None, which=0):
+        self.ends[...] = jnp.transpose(turned).reshape(nx, ny, nz)
+
+    def complete(self, slot, gains=None, which=0):
         nx, ny, nz = self.shape
         rx, ry, _ = self.landing
-        ends = self.ends(slot)
+        self.turn_ends(slot)
         for side, at in ((0, 0), (1, nx - 1)):
             other = rx[side, slot]
             if gains is not None:
@@ -160,24 +179,21 @@
             if gains is not None:
                 other = gains[2 + side, :, at : at + 1, :] * other
             self.partial[which, :, at : at + 1, :] = self.partial[which, :, at : at + 1, :] + other
-        if end_gain is not None:
-            ends = end_gain[...] * ends
-        return self.partial[which] + ends
-
-    def around(self, slot, field):
+
+    def pad_faces(self, slot):
+        nx, ny, _ = self.shape
+        rx, ry, _ = self.landing
+        self.ypad[0, 8 : 8 + ny, :] = rx[0, slot]
+        self.ypad[nx + 1, 8 : 8 + ny, :] = rx[1, slot]
+        self.ypad[1 : nx + 1, 7:8, :] = ry[0, slot]
+        self.ypad[1 : nx + 1, 8 + ny : 9 + ny, :] = ry[1, slot]
+
+    def clear_faces(self):
         nx, ny, nz = self.shape
-        rx, ry, _ = self.landing
-        below_x, above_x, below_y, above_y, below_z, above_z = self.inside(field)
-        below_x = jnp.concatenate([rx[0, slot][None], below_x[1:]], axis=0)
-        above_x = jnp.concatenate([above_x[:-1], rx[1, slot][None]], axis=0)
-        rows = lax.broadcasted_iota(jnp.int32, (nx, ny, nz), 1)
-        below_y = jnp.where(rows == 0, ry[0, slot], below_y)
-        above_y = jnp.where(rows == ny - 1, ry[1, slot], above_y)
-        lanes = lax.broadcasted_iota(jnp.int32, (nx, ny, nz), 2)
-        ends = self.ends(slot)
-        below_z = jnp.where(lanes == 0, ends, below_z)
-        above_z = jnp.where(lanes == nz - 1, ends, above_z)
-        return below_x, above_x, below_y, above_y, below_z, above_z
+        self.ypad[0] = jnp.zeros((ny + 16, nz), F32)
+        self.ypad[nx + 1] = jnp.zeros((ny + 16, nz), F32)
+        self.ypad[1 : nx + 1, 7:8, :] = jnp.zeros((nx, 1, nz), F32)
+        self.ypad[1 : nx + 1, 8 + ny : 9 + ny, :] = jnp.zeros((nx, 1, nz), F32)
 
 
 def total_of(parts):
@@ -262,12 +278,13 @@
     tsx, tsy, tsz, trx, try_, trz, typad, tsend, trecv,
     sent, arrived, returned, came,
     out_sem, in_sem, back_sem, home_sem,
-    hpart, tpart, end_gain, phi_h, source_h, current_h, gains, right_t, weight_t,
+    hpart, hends, update_h, tpart, tends, update_t, end_gain, conduct, phi_h, source_h,
+    current_h, gains, right_t, weight_t,
     rows_node, cols_node, rows_voxel, cols_voxel,
 ):
     n_grp, n_gx, n_gy = sizes
     peers = n_gx * n_gy
-    group = 8 if peers % 8 == 0 else 1
+    group = 2 if peers % 2 == 0 else 1
     g = lax.axis_index("grp")
     i = lax.axis_index("gx")
     j = lax.axis_index("gy")
@@ -302,8 +319,8 @@
         ("gy", (jnp.maximum(j - 1, 0), j > 0), (jnp.minimum(j + 1, n_gy - 1), j < n_gy - 1)),
         ("grp", (jnp.maximum(g - 1, 0), g > 0), (jnp.minimum(g + 1, n_grp - 1), g < n_grp - 1)),
     )
-    heart = Grid(hshape, (hsx, hsy, hsz), (hrx, hry, hrz), hsend, hrecv, hypad, place, hpart)
-    torso = Grid(tshape, (tsx, tsy, tsz), (trx, try_, trz), tsend, trecv, typad, place, tpart)
+    heart = Grid(hshape, (hsx, hsy, hsz), (hrx, hry, hrz), hsend, hrecv, hypad, place, hpart, hends, 4)
+    torso = Grid(tshape, (tsx, tsy, tsz), (trx, try_, trz), tsend, trecv, typad, place, tpart, tends, 2)
     heart.clear_ends()
     torso.clear_ends()
 
@@ -326,8 +343,7 @@
             pl.semaphore_signal(barrier, inc=1, device_id={"grp": there}, device_id_type=MESH)
 
     loads[0].wait()
-    voltage = membrane[...]
-    heart.pack(0, voltage)
+    heart.pack(0, membrane[...])
     loads[1].wait()
     heart.pack(1, phi_heart[...])
     pl.semaphore_wait(
@@ -337,32 +353,46 @@
 
     for load in loads[2:6]:
         load.wait()
-    names = labels[...]
-    table = jnp.where(names == 0, cond_table[0], 0.0)
-    for number in range(1, LABELS):
-        table = jnp.where(names == number, cond_table[number], table)
-    conduct = tissue_scale[...] * table
-    torso.pack(0, conduct)
+
+    def conductivity(at):
+        names = labels[at]
+        table = jnp.where(names == 0, cond_table[0], 0.0)
+        for number in range(1, LABELS):
+            table = jnp.where(names == number, cond_table[number], table)
+        conduct[at] = tissue_scale[at] * table
+
+    torso.planes(conductivity)
+    torso.pack(0, conduct[...])
     torso.pack(1, torso_phi[...])
     torso.send(0, 0, 2)
 
     def ionic(first, last):
-        voltage = membrane[...]
-        current = jnp.zeros(hshape, F32) if first == 0 else current_h[...]
-        for state in range(first, last):
-            line = jnp.zeros((1, 1, hshape[2]), F32)
-            half_slope = 0.5 / (line + ion_params[1, state])
-            decay = jnp.exp(line - time_step * ion_params[2, state])
-            steady = 0.5 + 0.5 * jnp.tanh((voltage - ion_params[0, state]) * half_slope)
-            gate = steady + (states[state].astype(F32) - steady) * decay
-            current = current + ion_params[3, state] * gate * (voltage - ion_params[4, state])
-        current_h[...] = current
-
-    heart.begin(voltage, which=0)
-    heart.begin(phi_heart[...], which=1)
-
-    ny = lax.broadcasted_iota(jnp.int32, hshape, 1) + j * hshape[1]
-    nz = lax.broadcasted_iota(jnp.int32, hshape, 2) + g * hshape[2]
+        line = jnp.zeros((1, hshape[2]), F32)
+        half_slopes = [0.5 / (line + ion_params[1, state]) for state in range(first, last)]
+        decays = [jnp.exp(line - time_step * ion_params[2, state]) for state in range(first, last)]
+
+        def body(at):
+            voltage = membrane[at]
+            current = jnp.zeros(hshape[1:], F32) if first == 0 else current_h[at]
+            for state in range(first, last):
+                half_slope, decay = half_slopes[state - first], decays[state - first]
+                steady = 0.5 + 0.5 * jnp.tanh((voltage - ion_params[0, state]) * half_slope)
+                gate = steady + (states[state, at].astype(F32) - steady) * decay
+                current = current + ion_params[3, state] * gate * (voltage - ion_params[4, state])
+            current_h[at] = current
+
+        heart.planes(body)
+
+    def fill(grid, ref):
+        grid.planes(lambda at: grid.put(at, ref[at]))
+
+    fill(heart, membrane)
+    heart.begin(which=0)
+    fill(heart, phi_heart)
+    heart.begin(which=1)
+
+    ny = lax.broadcasted_iota(jnp.int32, hshape[1:], 0) + j * hshape[1]
+    nz = lax.broadcasted_iota(jnp.int32, hshape[1:], 1) + g * hshape[2]
     diag = (
         6.0
         - jnp.where(ny == 0, 1.0, 0.0)
@@ -385,8 +415,6 @@
                 carry = body(number * group + offset, carry)
             return carry
 
-        if peers == group:
-            return one_group(0, start)
         return lax.fori_loop(0, peers // group, one_group, start)
 
     def indices():
@@ -398,49 +426,73 @@
             voxels.prepare(peer)
             return carry + voxels.weigh(peer)
 
-        weight_t[...] = penalty * over_peers(prepare, jnp.zeros((rows, width), F32))
+        weight = penalty * over_peers(prepare, jnp.zeros((rows, width), F32))
+        weight_t[0:layer] = weight.reshape(layer, tshape[1], width)
+        weight_t[layer:] = jnp.zeros((tshape[0] - layer,) + tshape[1:], F32)
 
     def conductances():
+        fill(torso, conduct)
         torso.wait(0, 0, 2)
-        faces = [harmonic(conduct, other) for other in torso.around(0, conduct)]
-        weight = weight_t[...].reshape(layer, tshape[1], width)
-        total = total_of(faces)
-        total = jnp.concatenate([total[:layer] + weight, total[layer:]], axis=0)
-        scale = 1.0 / total
-        for number in range(6):
-            gains[number] = faces[number] * scale
-        lanes = lax.broadcasted_iota(jnp.int32, tshape, 2)
-        end_gain[...] = jnp.where(
-            lanes == 0, faces[4] * scale, jnp.where(lanes == width - 1, faces[5] * scale, 0.0)
-        )
-        right_t[...] = penalty * scale[:layer]
+        torso.pad_faces(0)
+        torso.turn_ends(0)
+        lanes = lax.broadcasted_iota(jnp.int32, tshape[1:], 1)
+
+        def body(at):
+            plane = conduct[at]
+            ends = torso.ends[at]
+            parts = torso.inside(at)
+            parts[4] = parts[4] + jnp.where(lanes == 0, ends, 0.0)
+            parts[5] = parts[5] + jnp.where(lanes == width - 1, ends, 0.0)
+            faces = [harmonic(plane, part) for part in parts]
+            scale = 1.0 / (total_of(faces) + weight_t[at])
+            for number in range(6):
+                gains[number, at] = faces[number] * scale
+            end_gain[at] = jnp.where(
+                lanes == 0, faces[4] * scale, jnp.where(lanes == width - 1, faces[5] * scale, 0.0)
+            )
+            right_t[at] = penalty * scale
+
+        torso.planes(body)
+        torso.clear_faces()
 
     indices()
     heart.wait(0, 0, 2)
-    lap_mem = diag * voltage - heart.complete(0, which=0)
-    source_h[...] = lap_mem
-    base = (-intra_cond / (intra_cond + extra_cond)) * lap_mem * inverse
-    iterate = phi_heart[...]
-    update = None
+    heart.complete(0, which=0)
+
+    def laplacian(at):
+        source_h[at] = diag * membrane[at] - (heart.partial[0, at] + heart.ends[at])
+
+    heart.planes(laplacian)
+    from_lap = (-intra_cond / (intra_cond + extra_cond)) * inverse
     for number, (carry_coef, resid_coef) in enumerate(cheb_coeffs(SWEEPS_H)):
         if number > 0:
             heart.wait(number, number + 1, 1)
-        around = heart.complete(number + 1, which=1)
-        residue = base - iterate + around * inverse
-        update = resid_coef * residue if update is None else carry_coef * update + resid_coef * residue
-        iterate = iterate + update
+        heart.complete(number + 1, which=1)
+
+        def sweep(at, number=number, carry_coef=carry_coef, resid_coef=resid_coef):
+            iterate = heart.get(at)
+            around = heart.partial[1, at] + heart.ends[at]
+            residue = source_h[at] * from_lap - iterate + around * inverse
+            update = resid_coef * residue
+            if number > 0:
+                update = carry_coef * update_h[at] + update
+            update_h[at] = update
+            iterate = iterate + update
+            heart.put(at, iterate)
+            if number == SWEEPS_H - 1:
+                phi_h[at] = iterate
+
+        heart.planes(sweep)
         if number < SWEEPS_H - 1:
-            heart.pack(number + 2, iterate)
+            heart.pack(number + 2, heart.field())
             heart.send(number + 1, number + 2, 1)
-            heart.begin(iterate, which=1)
+            heart.begin(which=1)
         if number == 0:
             conductances()
         if number == 1:
-            torso.begin(torso_phi[...], gains)
-            partial = torso.complete(1, gains, end_gain)
-            tpart[0] = partial
-    phi_new = iterate
-    phi_h[...] = phi_new
+            fill(torso, torso_phi)
+            torso.begin(gains)
+            torso.complete(1, gains)
 
     def patch(other, source, target, sends, recvs, mine):
         return pltpu.make_async_remote_copy(
@@ -464,10 +516,7 @@
                 source[number * group + offset] = picked[offset]
             return carry
 
-        if peers == group:
-            one_group(0, 0)
-        else:
-            lax.fori_loop(0, peers // group, one_group, 0)
+        lax.fori_loop(0, peers // group, one_group, 0)
 
         def start(step, carry):
             patch(peer_at(step)[0], *buffers, me).start()
@@ -484,12 +533,12 @@
 
         lax.fori_loop(1, peers, land, 0, unroll=peers <= 8)
 
-    table_h = turned_table(phi_new[:layer_h], rows_h, hshape[2])
+    table_h = turned_table(phi_h[0:layer_h], rows_h, hshape[2])
     post(to_torso, lambda peer: nodes.pick(table_h, peer))
-    heart.pack(SWEEPS_H + 1, phi_new)
+    heart.pack(SWEEPS_H + 1, phi_h[...])
     heart.send(SWEEPS_H, SWEEPS_H + 1, 1)
 
-    heart.begin(phi_new, which=1)
+    heart.begin(which=1)
     half = states.shape[0] // 2
     loads[6].wait()
     loads[7].wait()
@@ -500,43 +549,53 @@
         jnp.zeros((rows, 2 * width), F32),
     )
     summed = summed[:, :width] + summed[:, width:]
-    right = summed.reshape(layer, tshape[1], width) * right_t[...]
-    right_t[...] = right
-
-    coeffs = cheb_coeffs(SWEEPS_T)
-    iterate = torso_phi[...]
-    update = tpart[0] - iterate
-    update = coeffs[0][1] * jnp.concatenate([update[:layer] + right, update[layer:]], axis=0)
-    iterate = iterate + update
-    for number in range(1, SWEEPS_T):
-        torso.pack(number + 1, iterate)
-        torso.send(number, number + 1, 1)
-        torso.begin(iterate, gains)
+    right_t[0:layer] = summed.reshape(layer, tshape[1], width) * right_t[0:layer]
+    right_t[layer:] = jnp.zeros((tshape[0] - layer,) + tshape[1:], F32)
+
+    for number, (carry_coef, resid_coef) in enumerate(cheb_coeffs(SWEEPS_T)):
+        if number > 0:
+            torso.pack(number + 1, torso.field())
+            torso.send(number, number + 1, 1)
+            torso.begin(gains)
         if number == 1:
             ionic(half, states.shape[0])
         if number == 2:
-            phi_new = phi_h[...]
             heart.wait(SWEEPS_H, SWEEPS_H + 1, 1)
-            lap_phi = diag * phi_new - heart.complete(SWEEPS_H + 1, which=1)
-            new_membrane[...] = membrane[...] + time_step * (
-                -intra_cond * (source_h[...] + lap_phi) - current_h[...]
-            )
+            heart.complete(SWEEPS_H + 1, which=1)
+
+            def depolarise(at):
+                lap_phi = diag * phi_h[at] - (heart.partial[1, at] + heart.ends[at])
+                new_membrane[at] = membrane[at] + time_step * (
+                    -intra_cond * (source_h[at] + lap_phi) - current_h[at]
+                )
+
+            heart.planes(depolarise)
             stores[0].start()
         if number == SWEEPS_T - 1:
             heart_phi[layer_h:] = phi_h[layer_h:]
             stores[2].start()
-        torso.wait(number, number + 1, 1)
-        residue = torso.complete(number + 1, gains, end_gain) - iterate
-        residue = jnp.concatenate([residue[:layer] + right_t[...], residue[layer:]], axis=0)
-        update = coeffs[number][0] * update + coeffs[number][1] * residue
-        iterate = iterate + update
-    table_t = turned_table(iterate[:layer], rows, width)
+        if number > 0:
+            torso.wait(number, number + 1, 1)
+            torso.complete(number + 1, gains)
+
+        def sweep_t(at, number=number, carry_coef=carry_coef, resid_coef=resid_coef):
+            iterate = torso.get(at)
+            around = torso.partial[0, at] + end_gain[at] * torso.ends[at]
+            update = resid_coef * (right_t[at] + (around - iterate))
+            if number > 0:
+                update = carry_coef * update_t[at] + update
+            update_t[at] = update
+            iterate = iterate + update
+            torso.put(at, iterate)
+            if number == SWEEPS_T - 1:
+                torso_out[at] = iterate
+
+        torso.planes(sweep_t)
+    table_t = turned_table(torso_out[0:layer], rows, width)
     post(
         to_heart, lambda peer: penalty * (arrived[peer] - voxels.pick(table_t, peer))
     )
-    torso_out[...] = iterate
     stores[1].start()
-    phi_new = phi_h[...]
 
     heart.finish(0, 0, 2)
     torso.finish(0, 0, 2)
@@ -551,8 +610,8 @@
         jnp.zeros((rows_h, 2 * hshape[2]), F32),
     )
     flux = (flux[:, : hshape[2]] + flux[:, hshape[2] :]).reshape(layer_h, hshape[1], hshape[2])
-    heart_phi[0:layer_h] = phi_new[:layer_h] - flux * (
-        inverse[:layer_h] * (1.0 / (intra_cond + extra_cond))
+    heart_phi[0:layer_h] = phi_h[0:layer_h] - flux * (
+        inverse * (1.0 / (intra_cond + extra_cond))
     )
     stores[3].start()
 
@@ -611,7 +670,7 @@
             faces
             + faces
             + [
-                pltpu.VMEM((nx, ny + 16, nz), F32),
+                pltpu.VMEM((nx + 2, ny + 16, nz), F32),
                 pltpu.SemaphoreType.DMA((turns, 3, 2)),
                 pltpu.SemaphoreType.DMA((turns, 3, 2)),
             ]
@@ -632,14 +691,19 @@
     rows = tx // 4 * ty
     work = [
         pltpu.VMEM((2,) + hshape, F32),
+        pltpu.VMEM(hshape, F32),
+        pltpu.VMEM(hshape, F32),
         pltpu.VMEM((1,) + tshape, F32),
+        pltpu.VMEM(tshape, F32),
+        pltpu.VMEM(tshape, F32),
+        pltpu.VMEM(tshape, F32),
         pltpu.VMEM(tshape, F32),
         pltpu.VMEM(hshape, F32),
         pltpu.VMEM(hshape, F32),
         pltpu.VMEM(hshape, F32),
         pltpu.VMEM((6, tx, ty, tz), F32),
-        pltpu.VMEM((tx // 4, ty, tz), F32),
-        pltpu.VMEM((rows, tz), F32),
+        pltpu.VMEM(tshape, F32),
+        pltpu.VMEM(tshape, F32),
         pltpu.VMEM((peers, rows_h, cap), BF16),
         pltpu.VMEM((peers, 1, cap), jnp.int32),
         pltpu.VMEM((peers, rows, cap), BF16),

time: 37.8 us -> 39.9 us (1.056)
  Pallas kernels: 37 us -> 39.1 us
    pallas_call x1, Pallas kernels: 35.2 us -> 37.2 us  [per_device(): pl.pallas_call(functools.partial(kernel, sizes), out_shape=shapes, in_spe...]
where the time goes in v4:
time: 39.9 us; the launch traced here: 39.7 us
  Pallas kernels  39.1 us (98%)
  between operations  0.64 us (2%)
    pallas_call x1, Pallas kernels, per_device(): pl.pallas_call(functools.partial(kernel, sizes), out_shape=shapes, in_spe...  37.2 us
    pallas_call x1, Pallas kernels, per_device(): pl.pallas_call(write_out, out_shape=shapes, in_specs=[hbm, hbm, hbm], out...  1.84 us

profile of v4, /device:TPU:0, one launch (start us, length us, event | category | flops | bytes accessed | tf_op | source)
XLA Modules:
  0.0 39.7 jit_solution(10149558986162082803)
XLA Ops:
  0.6 37.2 %shard_map.139 = (f32[16,16,128]{2,1,0:T(8,128)}, f32[16,16,128]{2,1,0:T(8,128)}, f32[16,32,128]{2,1,0:T(8,128)}) custom-call(bf16[12,16,16,128]{3,2,1,0:T(8,128)(2,1)} %states_in.1, f32[16,16,128]{2,1,0:T(8,128)} %membrane_in.1, f32[16,16,128]{2,1,0:T(8,128)} %phi_heart_in.1, f32[5,12]{1,0:T(8,128)} %ion_params_in.1, f32[16,32,128]{2,1,0:T(8,128)} %torso_phi_in.1, ...), custom_call_target="tpu_custom_call" | custom-call | tf_op jit(solution)/shard_map/pallas_call | solution.py:713
  37.9 1.8 %shard_map.140 = (f32[16,16,128]{2,1,0:T(8,128)}, f32[16,16,128]{2,1,0:T(8,128)}, f32[16,32,128]{2,1,0:T(8,128)}) custom-call(f32[16,16,128]{2,1,0:T(8,128)} %get-tuple-element.6.refs_0_, f32[16,16,128]{2,1,0:T(8,128)} %get-tuple-element.7.refs_1_, f32[16,32,128]{2,1,0:T(8,128)} %get-tuple-element.8.refs_2_), custom_call_target="tpu_custom_call" | custom-call | tf_op jit(solution)/shard_map/pallas_call | solution.py:728

commit v5 on v3

--- a/solution.py
+++ b/solution.py
@@ -415,7 +415,6 @@
         )
         right_t[...] = penalty * scale[:layer]
 
-    indices()
     heart.wait(0, 0, 2)
     lap_mem = diag * voltage - heart.complete(0, which=0)
     source_h[...] = lap_mem
@@ -434,11 +433,9 @@
             heart.send(number + 1, number + 2, 1)
             heart.begin(iterate, which=1)
         if number == 0:
+            indices()
+        if number == 1:
             conductances()
-        if number == 1:
-            torso.begin(torso_phi[...], gains)
-            partial = torso.complete(1, gains, end_gain)
-            tpart[0] = partial
     phi_new = iterate
     phi_h[...] = phi_new
 
@@ -489,11 +486,9 @@
     heart.pack(SWEEPS_H + 1, phi_new)
     heart.send(SWEEPS_H, SWEEPS_H + 1, 1)
 
-    heart.begin(phi_new, which=1)
-    half = states.shape[0] // 2
-    loads[6].wait()
-    loads[7].wait()
-    ionic(0, half)
+    torso.begin(torso_phi[...], gains)
+    partial = torso.complete(1, gains, end_gain)
+    tpart[0] = partial
     receive(to_torso)
     summed = over_peers(
         lambda peer, carry: carry + voxels.place_at(arrived[peer], peer),
@@ -513,18 +508,11 @@
         torso.send(number, number + 1, 1)
         torso.begin(iterate, gains)
         if number == 1:
-            ionic(half, states.shape[0])
-        if number == 2:
-            phi_new = phi_h[...]
-            heart.wait(SWEEPS_H, SWEEPS_H + 1, 1)
-            lap_phi = diag * phi_new - heart.complete(SWEEPS_H + 1, which=1)
-            new_membrane[...] = membrane[...] + time_step * (
-                -intra_cond * (source_h[...] + lap_phi) - current_h[...]
-            )
-            stores[0].start()
-        if number == SWEEPS_T - 1:
-            heart_phi[layer_h:] = phi_h[layer_h:]
-            stores[2].start()
+            heart.begin(phi_h[...], which=1)
+            loads[6].wait()
+            loads[7].wait()
+        count = states.shape[0]
+        ionic(count * (number - 1) // (SWEEPS_T - 1), count * number // (SWEEPS_T - 1))
         torso.wait(number, number + 1, 1)
         residue = torso.complete(number + 1, gains, end_gain) - iterate
         residue = jnp.concatenate([residue[:layer] + right_t[...], residue[layer:]], axis=0)
@@ -537,6 +525,14 @@
     torso_out[...] = iterate
     stores[1].start()
     phi_new = phi_h[...]
+    heart_phi[layer_h:] = phi_new[layer_h:]
+    stores[2].start()
+    heart.wait(SWEEPS_H, SWEEPS_H + 1, 1)
+    lap_phi = diag * phi_new - heart.complete(SWEEPS_H + 1, which=1)
+    new_membrane[...] = membrane[...] + time_step * (
+        -intra_cond * (source_h[...] + lap_phi) - current_h[...]
+    )
+    stores[0].start()
 
     heart.finish(0, 0, 2)
     torso.finish(0, 0, 2)

time: 37.8 us -> 37.8 us (level)
  no operation moved by 1% of the time
where the time goes in v5:
time: 37.8 us; the launch traced here: 37.7 us
  Pallas kernels  37 us (98%)
  between operations  0.64 us (2%)
    pallas_call x1, Pallas kernels, per_device(): pl.pallas_call(functools.partial(kernel, sizes), out_shape=shapes, in_spe...  35.2 us
    pallas_call x1, Pallas kernels, per_device(): pl.pallas_call(write_out, out_shape=shapes, in_specs=[hbm, hbm, hbm], out...  1.84 us

profile of v5, /device:TPU:0, one launch (start us, length us, event | category | flops | bytes accessed | tf_op | source)
XLA Modules:
  0.0 37.7 jit_solution(14818105303059416016)
XLA Ops:
  0.6 35.2 %shard_map.139 = (f32[16,16,128]{2,1,0:T(8,128)}, f32[16,16,128]{2,1,0:T(8,128)}, f32[16,32,128]{2,1,0:T(8,128)}) custom-call(bf16[12,16,16,128]{3,2,1,0:T(8,128)(2,1)} %states_in.1, f32[16,16,128]{2,1,0:T(8,128)} %membrane_in.1, f32[16,16,128]{2,1,0:T(8,128)} %phi_heart_in.1, f32[5,12]{1,0:T(8,128)} %ion_params_in.1, f32[16,32,128]{2,1,0:T(8,128)} %torso_phi_in.1, ...), custom_call_target="tpu_custom_call" | custom-call | tf_op jit(solution)/shard_map/pallas_call | solution.py:645
  35.8 1.8 %shard_map.140 = (f32[16,16,128]{2,1,0:T(8,128)}, f32[16,16,128]{2,1,0:T(8,128)}, f32[16,32,128]{2,1,0:T(8,128)}) custom-call(f32[16,16,128]{2,1,0:T(8,128)} %get-tuple-element.6.refs_0_, f32[16,16,128]{2,1,0:T(8,128)} %get-tuple-element.7.refs_1_, f32[16,32,128]{2,1,0:T(8,128)} %get-tuple-element.8.refs_2_), custom_call_target="tpu_custom_call" | custom-call | tf_op jit(solution)/shard_map/pallas_call | solution.py:660

commit v6 on v5

--- a/solution.py
+++ b/solution.py
@@ -77,9 +77,18 @@
         xs[1, slot] = field[nx - 1]
         ys[0, slot] = field[:, 0:1, :]
         ys[1, slot] = field[:, ny - 1 : ny, :]
-        turned = jnp.transpose(field.reshape(nx * ny, nz))
-        zs[0, slot] = turned[0:1, :]
-        zs[1, slot] = turned[nz - 1 : nz, :]
+        tiles = field.reshape(nx * ny // 8, 8, nz)
+        lanes = lax.broadcasted_iota(jnp.int32, (8, nz), 1)
+        pairs = lax.shift_right_logical((lanes + 1) & (nz - 1), 1)
+        sums = [jnp.zeros((8, nz), F32) for _ in range(4)]
+        for number in range(nx * ny // 8):
+            tile = tiles[number]
+            if number > 0:
+                tile = pltpu.roll(tile, 2 * number, 1)
+            sums[number % 4] = jnp.where(pairs == number, tile, sums[number % 4])
+        both = (sums[0] + sums[1]) + (sums[2] + sums[3])
+        zs[0, slot] = both
+        zs[1, slot] = both
 
     def copies(self, turn, first, count):
         for axis, (name, low, high) in enumerate(self.place):
@@ -142,9 +151,14 @@
     def ends(self, slot):
         nx, ny, nz = self.shape
         rz = self.landing[2]
-        depth = lax.broadcasted_iota(jnp.int32, (nz, nx * ny), 0)
-        turned = jnp.where(depth == 0, rz[0, slot], jnp.where(depth == nz - 1, rz[1, slot], 0.0))
-        return jnp.transpose(turned).reshape(nx, ny, nz)
+        lanes = lax.broadcasted_iota(jnp.int32, (8, nz), 1)
+        both = jnp.where(
+            lanes & 1 == 0, pltpu.roll(rz[0, slot], 1, 1), pltpu.roll(rz[1, slot], nz - 1, 1)
+        )
+        tiles = [both] + [
+            pltpu.roll(both, nz - 2 * number, 1) for number in range(1, nx * ny // 8)
+        ]
+        return jnp.concatenate(tiles, axis=0).reshape(nx, ny, nz)
 
     def complete(self, slot, gains=None, end_gain=None, which=0):
         nx, ny, nz = self.shape
@@ -162,6 +176,9 @@
             self.partial[which, :, at : at + 1, :] = self.partial[which, :, at : at + 1, :] + other
         if end_gain is not None:
             ends = end_gain[...] * ends
+        else:
+            lanes = lax.broadcasted_iota(jnp.int32, (nx, ny, nz), 2)
+            ends = jnp.where((lanes == 0) | (lanes == nz - 1), ends, 0.0)
         return self.partial[which] + ends
 
     def around(self, slot, field):
@@ -601,7 +618,7 @@
         faces = [
             pltpu.VMEM((2, slots, ny, nz), F32),
             pltpu.VMEM((2, slots, nx, 1, nz), F32),
-            pltpu.VMEM((2, slots, 1, nx * ny), F32),
+            pltpu.VMEM((2, slots, 8, nz), F32),
         ]
         return (
             faces

time: 37.8 us -> 38.3 us (1.013)
  Pallas kernels: 37 us -> 37.5 us
    pallas_call x1, Pallas kernels: 35.2 us -> 35.6 us  [per_device(): pl.pallas_call(functools.partial(kernel, sizes), out_shape=shapes, in_spe...]
where the time goes in v6:
time: 38.3 us; the launch traced here: 38.1 us
  Pallas kernels  37.5 us (98%)
  between operations  0.64 us (2%)
    pallas_call x1, Pallas kernels, per_device(): pl.pallas_call(functools.partial(kernel, sizes), out_shape=shapes, in_spe...  35.6 us
    pallas_call x1, Pallas kernels, per_device(): pl.pallas_call(write_out, out_shape=shapes, in_specs=[hbm, hbm, hbm], out...  1.84 us

profile of v6, /device:TPU:0, one launch (start us, length us, event | category | flops | bytes accessed | tf_op | source)
XLA Modules:
  0.0 38.1 jit_solution(13396561058590123202)
XLA Ops:
  0.6 35.6 %shard_map.139 = (f32[16,16,128]{2,1,0:T(8,128)}, f32[16,16,128]{2,1,0:T(8,128)}, f32[16,32,128]{2,1,0:T(8,128)}) custom-call(bf16[12,16,16,128]{3,2,1,0:T(8,128)(2,1)} %states_in.1, f32[16,16,128]{2,1,0:T(8,128)} %membrane_in.1, f32[16,16,128]{2,1,0:T(8,128)} %phi_heart_in.1, f32[5,12]{1,0:T(8,128)} %ion_params_in.1, f32[16,32,128]{2,1,0:T(8,128)} %torso_phi_in.1, ...), custom_call_target="tpu_custom_call" | custom-call | tf_op jit(solution)/shard_map/pallas_call | solution.py:662
  36.3 1.8 %shard_map.140 = (f32[16,16,128]{2,1,0:T(8,128)}, f32[16,16,128]{2,1,0:T(8,128)}, f32[16,32,128]{2,1,0:T(8,128)}) custom-call(f32[16,16,128]{2,1,0:T(8,128)} %get-tuple-element.6.refs_0_, f32[16,16,128]{2,1,0:T(8,128)} %get-tuple-element.7.refs_1_, f32[16,32,128]{2,1,0:T(8,128)} %get-tuple-element.8.refs_2_), custom_call_target="tpu_custom_call" | custom-call | tf_op jit(solution)/shard_map/pallas_call | solution.py:677

commit v7 on v5

--- a/solution.py
+++ b/solution.py
@@ -455,31 +455,25 @@
     def post(buffers, fill):
         source, target = buffers[:2]
 
-        def one_group(number, carry):
-            picked = [fill(number * group + offset) for offset in range(group)]
-            for offset in range(group):
-                source[number * group + offset] = picked[offset]
+        def start(step, carry):
+            other = peer_at(step)[0]
+            source[other] = fill(other)
+            patch(other, *buffers, me).start()
             return carry
 
-        if peers == group:
-            one_group(0, 0)
-        else:
-            lax.fori_loop(0, peers // group, one_group, 0)
-
-        def start(step, carry):
-            patch(peer_at(step)[0], *buffers, me).start()
-            return carry
-
         lax.fori_loop(1, peers, start, 0, unroll=peers <= 8)
-        target[me] = source[me]
-
-    def receive(buffers):
+        target[me] = fill(me)
+
+    def receive(buffers, spots, start):
+        target = buffers[1]
+
         def land(step, carry):
             other = peer_at(step)[0]
             patch(other, *buffers, other).wait_recv()
-            return carry
-
-        lax.fori_loop(1, peers, land, 0, unroll=peers <= 8)
+            return carry + spots.place_at(target[other], other)
+
+        own = start + spots.place_at(target[me], me)
+        return lax.fori_loop(1, peers, land, own, unroll=peers <= 8)
 
     table_h = turned_table(phi_new[:layer_h], rows_h, hshape[2])
     post(to_torso, lambda peer: nodes.pick(table_h, peer))
@@ -489,11 +483,7 @@
     torso.begin(torso_phi[...], gains)
     partial = torso.complete(1, gains, end_gain)
     tpart[0] = partial
-    receive(to_torso)
-    summed = over_peers(
-        lambda peer, carry: carry + voxels.place_at(arrived[peer], peer),
-        jnp.zeros((rows, 2 * width), F32),
-    )
+    summed = receive(to_torso, voxels, jnp.zeros((rows, 2 * width), F32))
     summed = summed[:, :width] + summed[:, width:]
     right = summed.reshape(layer, tshape[1], width) * right_t[...]
     right_t[...] = right
@@ -541,11 +531,7 @@
     for number in range(1, SWEEPS_T):
         torso.finish(number, number + 1, 1)
 
-    receive(to_heart)
-    flux = over_peers(
-        lambda peer, carry: carry + nodes.place_at(came[peer], peer),
-        jnp.zeros((rows_h, 2 * hshape[2]), F32),
-    )
+    flux = receive(to_heart, nodes, jnp.zeros((rows_h, 2 * hshape[2]), F32))
     flux = (flux[:, : hshape[2]] + flux[:, hshape[2] :]).reshape(layer_h, hshape[1], hshape[2])
     heart_phi[0:layer_h] = phi_new[:layer_h] - flux * (
         inverse[:layer_h] * (1.0 / (intra_cond + extra_cond))

time: 37.8 us -> 38.9 us (1.029)
  Pallas kernels: 37 us -> 38.1 us
    pallas_call x1, Pallas kernels: 35.2 us -> 36.2 us  [per_device(): pl.pallas_call(functools.partial(kernel, sizes), out_shape=shapes, in_spe...]
where the time goes in v7:
time: 38.9 us; the launch traced here: 38.7 us
  Pallas kernels  38.1 us (98%)
  between operations  0.64 us (2%)
    pallas_call x1, Pallas kernels, per_device(): pl.pallas_call(functools.partial(kernel, sizes), out_shape=shapes, in_spe...  36.2 us
    pallas_call x1, Pallas kernels, per_device(): pl.pallas_call(write_out, out_shape=shapes, in_specs=[hbm, hbm, hbm], out...  1.84 us

profile of v7, /device:TPU:0, one launch (start us, length us, event | category | flops | bytes accessed | tf_op | source)
XLA Modules:
  0.0 38.7 jit_solution(3882355485723419582)
XLA Ops:
  0.6 36.2 %shard_map.139 = (f32[16,16,128]{2,1,0:T(8,128)}, f32[16,16,128]{2,1,0:T(8,128)}, f32[16,32,128]{2,1,0:T(8,128)}) custom-call(bf16[12,16,16,128]{3,2,1,0:T(8,128)(2,1)} %states_in.1, f32[16,16,128]{2,1,0:T(8,128)} %membrane_in.1, f32[16,16,128]{2,1,0:T(8,128)} %phi_heart_in.1, f32[5,12]{1,0:T(8,128)} %ion_params_in.1, f32[16,32,128]{2,1,0:T(8,128)} %torso_phi_in.1, ...), custom_call_target="tpu_custom_call" | custom-call | tf_op jit(solution)/shard_map/pallas_call | solution.py:631
  36.9 1.8 %shard_map.140 = (f32[16,16,128]{2,1,0:T(8,128)}, f32[16,16,128]{2,1,0:T(8,128)}, f32[16,32,128]{2,1,0:T(8,128)}) custom-call(f32[16,16,128]{2,1,0:T(8,128)} %get-tuple-element.6.refs_0_, f32[16,16,128]{2,1,0:T(8,128)} %get-tuple-element.7.refs_1_, f32[16,32,128]{2,1,0:T(8,128)} %get-tuple-element.8.refs_2_), custom_call_target="tpu_custom_call" | custom-call | tf_op jit(solution)/shard_map/pallas_call | solution.py:646
